TPU v7x, 256 devices: a whole 4x4x8 slice. The times are simulated.
256 devices in a mesh: ctx: 64 (over z_hi, x, y, core), tp: 4 (over z_lo).
Axes of the slice: x: 4, y: 4, z: 8 (z_hi: 2, z_lo: 4; z = z_hi * 4 + z_lo), core: 2. Of those that a mesh axis runs over, the one named last changes fastest.
Arguments:
- queries: bfloat16 [8192, 4096], P(('ctx', 'tp')), may hold values from -180 to 180
- keys: bfloat16 [8192, 512], P(('ctx', 'tp')), may hold values from -6 to 6
- values: bfloat16 [8192, 512], P(('ctx', 'tp')), may hold values from -6 to 6
- out_grad: bfloat16 [8192, 4096], P(('ctx', 'tp')), may hold values from -6 to 6
- doc_lengths: int32 [16], replicated, may hold values from 1 to 2048, 8192 in all
- row_block: int32 [128], replicated, may hold values from 0 to 127, as said below
Outputs:
- attended: bfloat16 [8192, 4096], P(('ctx', 'tp'))
- query_grad: bfloat16 [8192, 4096], P(('ctx', 'tp'))
- key_grad: bfloat16 [8192, 512], P(('ctx', 'tp'))
- value_grad: bfloat16 [8192, 512], P(('ctx', 'tp'))
Inputs may be any that keep to these rules, and one draw needn't show every extreme that they name: `doc_lengths`: they add up to 8192; the longest is exactly 2048. `row_block`: each block number appears once; the two slots 2c and 2c + 1 of context shard c hold blocks k and 127 - k for some k.
All inputs are finite; a program needn't handle non-finite values.
Results may differ from a plain program's by a relative error of at most 0.039.
Values may be sent and summed in bfloat16 or wider, within the bound.
A program may use at most 64 MiB of HBM per device.

v0:
```python
import math

import jax
import jax.numpy as jnp
from jax import lax
from jax.sharding import PartitionSpec as P

HEAD = 128


negative = -1e30
block_span = 512


def locate(row_block, doc_lengths, block_rows):
    offsets = jnp.arange(block_rows, dtype=jnp.int32)
    positions = (row_block[:, None] * block_rows + offsets[None, :]).reshape(-1)
    ends = jnp.cumsum(doc_lengths)
    documents = jnp.sum((positions[:, None] >= ends[None, :]).astype(jnp.int32), axis=1)
    return (positions, documents)


def split_heads(piece, kv_local):
    return piece.reshape(piece.shape[0], kv_local, -1)


def over_blocks(step, carry, key_part, value_part):
    count = key_part.shape[0]
    pieces = count // block_span
    key_split = key_part.reshape(pieces, block_span, key_part.shape[1])
    value_split = value_part.reshape(pieces, block_span, value_part.shape[1])

    def inner(state, item):
        number, key_block, value_block = item
        return (step(state, key_block, value_block, number * block_span), None)

    carry, unused = lax.scan(
        inner, carry, (jnp.arange(pieces, dtype=jnp.int32), key_split, value_split)
    )
    return carry


def per_device(queries, keys, values, out_grad, doc_lengths, row_block):
    q_local, k_local, v_local, g_local = (
        lax.all_to_all(queries, "tp", split_axis=1, concat_axis=0, tiled=True),
        lax.all_to_all(keys, "tp", split_axis=1, concat_axis=0, tiled=True),
        lax.all_to_all(values, "tp", split_axis=1, concat_axis=0, tiled=True),
        lax.all_to_all(out_grad, "tp", split_axis=1, concat_axis=0, tiled=True),
    )
    rows = q_local.shape[0]
    kv_width = k_local.shape[1]
    kv_local = kv_width // HEAD
    group = q_local.shape[1] // kv_width
    seq_rows = rows * lax.axis_size("ctx")
    scale = 1.0 / math.sqrt(HEAD)
    q_four = q_local.reshape(rows, kv_local, group, HEAD)
    positions, documents = locate(row_block, doc_lengths, rows // 2)
    first_row = lax.axis_index("ctx") * rows
    query_pos = lax.dynamic_slice_in_dim(positions, first_row, rows)
    query_doc = lax.dynamic_slice_in_dim(documents, first_row, rows)

    def mask_for(start, count):
        key_pos = lax.dynamic_slice_in_dim(positions, start, count)
        key_doc = lax.dynamic_slice_in_dim(documents, start, count)
        seen = (key_pos[None, :] <= query_pos[:, None]) & (key_doc[None, :] == query_doc[:, None])
        return seen[None, None]

    def forward_step(state, key_block, value_block, start):
        top, total, accum = state
        mask = mask_for(start, key_block.shape[0])
        scores = (
            jnp.einsum(
                "tkgd,skd->kgts",
                q_four,
                split_heads(key_block, kv_local),
                preferred_element_type=jnp.float32,
            )
            * scale
        )
        scores = jnp.where(mask, scores, negative)
        new_top = jnp.maximum(top, jnp.max(scores, axis=-1))
        factor = jnp.exp(top - new_top)
        weights = jnp.where(mask, jnp.exp(scores - new_top[..., None]), 0.0)
        total = factor * total + jnp.sum(weights, axis=-1)
        product = jnp.einsum(
            "kgts,skd->kgtd",
            weights.astype(jnp.bfloat16),
            split_heads(value_block, kv_local),
            preferred_element_type=jnp.float32,
        )
        accum = factor[..., None] * accum + product
        return (new_top, total, accum)

    stat_shape = (kv_local, group, rows)
    start_state = (
        jnp.full(stat_shape, negative, jnp.float32),
        jnp.zeros(stat_shape, jnp.float32),
        jnp.zeros(stat_shape + (HEAD,), jnp.float32),
    )
    piece = (
        lax.all_gather(k_local, "ctx", axis=0, tiled=True),
        lax.all_gather(v_local, "ctx", axis=0, tiled=True),
    )
    top, total, accum = over_blocks(forward_step, start_state, piece[0], piece[1])
    log_total = top + jnp.log(total)
    attended = (accum / total[..., None]).astype(jnp.bfloat16)
    attended_rows = attended.transpose(2, 0, 1, 3).reshape(rows, -1)
    g_four = g_local.reshape(rows, kv_local, group, HEAD)
    delta = jnp.einsum("tkgd,kgtd->kgt", g_four, attended, preferred_element_type=jnp.float32)

    def backward_step(state, key_block, value_block, start):
        query_acc, key_acc, value_acc = state
        count = key_block.shape[0]
        mask = mask_for(start, count)
        key_three = split_heads(key_block, kv_local)
        scores = (
            jnp.einsum("tkgd,skd->kgts", q_four, key_three, preferred_element_type=jnp.float32)
            * scale
        )
        probs = jnp.where(mask, jnp.exp(scores - log_total[..., None]), 0.0)
        d_probs = jnp.einsum(
            "tkgd,skd->kgts",
            g_four,
            split_heads(value_block, kv_local),
            preferred_element_type=jnp.float32,
        )
        d_scores = (probs * (d_probs - delta[..., None]) * scale).astype(jnp.bfloat16)
        query_acc = query_acc + jnp.einsum(
            "kgts,skd->kgtd", d_scores, key_three, preferred_element_type=jnp.float32
        )
        key_part = jnp.einsum(
            "kgts,tkgd->skd", d_scores, q_four, preferred_element_type=jnp.float32
        ).reshape(count, -1)
        value_part = jnp.einsum(
            "kgts,tkgd->skd", probs.astype(jnp.bfloat16), g_four, preferred_element_type=jnp.float32
        ).reshape(count, -1)
        key_acc = lax.dynamic_update_slice_in_dim(
            key_acc, lax.dynamic_slice_in_dim(key_acc, start, count, 0) + key_part, start, 0
        )
        value_acc = lax.dynamic_update_slice_in_dim(
            value_acc, lax.dynamic_slice_in_dim(value_acc, start, count, 0) + value_part, start, 0
        )
        return (query_acc, key_acc, value_acc)

    grad_start = (
        jnp.zeros(stat_shape + (HEAD,), jnp.float32),
        jnp.zeros((seq_rows, kv_width), jnp.float32),
        jnp.zeros((seq_rows, kv_width), jnp.float32),
    )
    piece = (
        lax.all_gather(k_local, "ctx", axis=0, tiled=True),
        lax.all_gather(v_local, "ctx", axis=0, tiled=True),
    )
    query_acc, key_acc, value_acc = over_blocks(backward_step, grad_start, piece[0], piece[1])
    key_mine, value_mine = (
        lax.psum_scatter(key_acc, "ctx", scatter_dimension=0, tiled=True),
        lax.psum_scatter(value_acc, "ctx", scatter_dimension=0, tiled=True),
    )
    query_grad = query_acc.astype(jnp.bfloat16).transpose(2, 0, 1, 3).reshape(rows, -1)
    results = (
        lax.all_to_all(attended_rows, "tp", split_axis=0, concat_axis=1, tiled=True),
        lax.all_to_all(query_grad, "tp", split_axis=0, concat_axis=1, tiled=True),
        lax.all_to_all(
            key_mine.astype(jnp.bfloat16), "tp", split_axis=0, concat_axis=1, tiled=True
        ),
        lax.all_to_all(
            value_mine.astype(jnp.bfloat16), "tp", split_axis=0, concat_axis=1, tiled=True
        ),
    )
    return (results[0], results[1], results[2], results[3])


def solution(mesh):
    return jax.shard_map(
        per_device,
        mesh=mesh,
        in_specs=(
            P(("ctx", "tp"), None),
            P(("ctx", "tp"), None),
            P(("ctx", "tp"), None),
            P(("ctx", "tp"), None),
            P(),
            P(),
        ),
        out_specs=(
            P(("ctx", "tp"), None),
            P(("ctx", "tp"), None),
            P(("ctx", "tp"), None),
            P(("ctx", "tp"), None),
        ),
        check_vma=False,
    )
```

profile of v0, /device:TPU:1, one launch (start us, length us, event | category | flops | bytes accessed | tf_op | source)
XLA Modules:
  0.0 1273.3 jit_solution(9398726847674755434)
XLA Ops:
  7.9 10.8 all_to_all.146
  19.6 7.5 all_to_all.147
  28.8 3.4 all-to-all-start.1
  33.9 4.3 all-to-all-done.1
  38.3 3.4 all-to-all-start.4
  42.6 4.6 all-to-all-done.4
  47.4 56.7 %all-gather.3.cloned.1.call-done = bf16[8192,128]{1,0:T(8,128)(2,1)} async-done(((bf16[128,128]{1,0:T(8,128)(2,1)}), bf16[8192,128]{1,0:T(8,128)(2,1)}) %all-gather.3.cloned.1.call-update) | async-done | bytes 2097168 | tf_op jit(solution)/shard_map/all_gather | solution.py:101
  104.1 80.4 %all-gather.5.cloned.1.call-done = bf16[8192,128]{1,0:T(8,128)(2,1)} async-done(((bf16[128,128]{1,0:T(8,128)(2,1)}), bf16[8192,128]{1,0:T(8,128)(2,1)}) %all-gather.5.cloned.1.call-update) | async-done | bytes 2097168 | tf_op jit(solution)/shard_map/all_gather | solution.py:102
  184.5 85.1 %while.30 = (s32[]{:T(128)}, f32[1,8,128]{2,1,0:T(8,128)S(1)}, f32[1,8,128]{2,1,0:T(8,128)S(1)}, f32[1,8,128,128]{3,2,1,0:T(8,128)S(1)}, s32[16]{0:T(128)S(1)}, ...) while((s32[]{:T(128)}, f32[1,8,128]{2,1,0:T(8,128)S(1)}, ...), condition=%wide.region_5.6_spmd.clone, body=%wide.region_2.5_spmd.clone.sunk | while | flops 275847168 | bytes 8205555 | solution.py:37
  270.3 2.3 broadcast.114.clone
  272.6 2.2 broadcast.114
  274.8 163.4 %while.31 = (s32[]{:T(128)}, f32[1,8,128,128]{3,2,1,0:T(8,128)S(1)}, f32[8192,128]{1,0:T(8,128)}, f32[8192,128]{1,0:T(8,128)}, s32[16]{0:T(128)S(1)}, /*index=5*...) while((s32[]{:T(128)}, ...), condition=%wide.region_7.8_spmd.clone, body=%wide.region_6.7_spmd.clone.sunk | while | flops 675872768 | bytes 13128981 | solution.py:37
  291.0 2.1 fusion.97
  321.7 2.1 fusion.97
  393.1 2.1 fusion.97
  434.0 2.2 fusion.97
  439.8 3.4 all-to-all-start.3
  444.3 7.5 all-to-all-done.3
  451.8 3.5 all-to-all-start.5
  455.4 386.2 %reduce-scatter.3.cloned.1.call-done = f32[128,128]{1,0:T(8,128)} async-done(((f32[8192,128]{1,0:T(8,128)}), f32[128,128]{1,0:T(8,128)}) %reduce-scatter.3.cloned.1.call-update) | async-done | bytes 65552 | tf_op jit(solution)/shard_map/reduce_scatter | solution.py:156
  843.1 4.2 all-to-all-start.6
  848.7 407.4 %reduce-scatter.5.cloned.1.call-done = f32[128,128]{1,0:T(8,128)} async-done(((f32[8192,128]{1,0:T(8,128)}), f32[128,128]{1,0:T(8,128)}) %reduce-scatter.5.cloned.1.call-update) | async-done | bytes 65552 | tf_op jit(solution)/shard_map/reduce_scatter | solution.py:157
  1257.6 4.1 all-to-all-start.7
  1262.2 3.9 all-to-all-done.7
  (354 shorter events, 232.2 us)
Async XLA Ops:
  7.2 0.8 copy-start
  7.2 34.5 %copy-start.2 = (s32[128]{0:T(128)S(1)}, s32[128]{0:T(128)}, u32[]{:S(2)}) copy-start(s32[128]{0:T(128)} %param.15) | copy-start | bytes 1540
  7.2 34.6 %copy-start.1 = (s32[16]{0:T(128)S(1)}, s32[16]{0:T(128)}, u32[]{:S(2)}) copy-start(s32[16]{0:T(128)} %param.14) | copy-start | bytes 196
  7.2 96.9 %all-gather.3.cloned.1.call-start = ((), (), s32[]{:S(2)}) async-start(), calls=%async_computation.10 | async-start | bytes 2129920 | tf_op jit(solution)/shard_map/all_gather | solution.py:101
  18.8 165.7 %all-gather.5.cloned.1.call-start = ((), (), s32[]{:S(2)}) async-start(), calls=%async_computation.11 | async-start | bytes 2129920 | tf_op jit(solution)/shard_map/all_gather | solution.py:102
  28.8 9.4 all-to-all-start.1
  38.3 9.0 all-to-all-start.4
  41.7 799.9 %reduce-scatter.3.cloned.1.call-start = ((), (), s32[]{:S(2)}) async-start(), calls=%async_computation.12 | async-start | bytes 4259840 | tf_op jit(solution)/shard_map/reduce_scatter | solution.py:156
  438.3 817.9 %reduce-scatter.5.cloned.1.call-start = ((), (), s32[]{:S(2)}) async-start(), calls=%async_computation.13 | async-start | bytes 4259840 | tf_op jit(solution)/shard_map/reduce_scatter | solution.py:157
  439.8 12.0 all-to-all-start.3
  451.8 391.2 %all-to-all-start.5 = ((bf16[4,32,1024]{2,1,0:T(8,128)(2,1)}), bf16[4,32,1024]{2,1,0:T(8,128)(2,1)S(1)}, u32[]{:S(2)}, u32[]{:S(2)}) async-start(bf16[4,32,1024]{2,1,0:T(8,128)(2,1)} %all_to_all.126), calls=%async_computation.5 | async-start | bytes 524288 | tf_op jit(solution)/shard_map/all_to_all | solution.py:162
  843.1 414.5 %all-to-all-start.6 = ((bf16[4,32,128]{2,1,0:T(8,128)(2,1)}), bf16[4,32,128]{2,1,0:T(8,128)(2,1)S(1)}, u32[]{:S(2)}, u32[]{:S(2)}) async-start(bf16[4,32,128]{2,1,0:T(8,128)(2,1)} %bitcast.17), calls=%async_computation.7 | async-start | bytes 65536 | tf_op jit(solution)/shard_map/all_to_all | solution.py:163
  1257.6 8.6 all-to-all-start.7
Sparse Core Ops, SparseCore 0:
  18.9 85.0 all-gather.2
  107.6 76.8 all-gather.4
  438.4 403.1 reduce-scatter.2
  844.1 411.9 reduce-scatter.4
where the time goes:
time: 1290 us; the launch traced here: 1270 us
  waiting for transfers between devices  952 us (74%)
  matrix products  187 us (14%)
  local copies, waits for them, and re-layouts  38.1 us (3%)
  loops' own time  22.5 us (2%)
  starting transfers between devices  22.2 us (2%)
  other arithmetic  19.2 us (1%)
  blocking collectives  18.4 us (1%)
  between operations  14 us (1%)
    reduce_scatter x1, waiting for transfers between devices, per_device(): lax.psum_scatter(value_acc, 'ctx', scatter_dimension=0, tiled=True)  407 us
    reduce_scatter x1, waiting for transfers between devices, per_device(): lax.psum_scatter(key_acc, 'ctx', scatter_dimension=0, tiled=True)  386 us
    all_gather x1, waiting for transfers between devices, per_device(): lax.all_gather(v_local, 'ctx', axis=0, tiled=True)  80.4 us
    all_gather x1, waiting for transfers between devices, per_device(): lax.all_gather(k_local, 'ctx', axis=0, tiled=True)  56.7 us
    dot_general x16, matrix products, backward_step(): jnp.einsum('kgts,tkgd->skd', probs.astype(jnp.bfloat16), g_four, preferre...  33.7 us
    dot_general x16, matrix products, backward_step(): jnp.einsum('kgts,tkgd->skd', d_scores, q_four, preferred_element_type=jnp...  33.5 us
    dot_general x16, matrix products, forward_step(): jnp.einsum('kgts,skd->kgtd', weights.astype(jnp.bfloat16), split_heads(va...  28.1 us
  transfers between devices with their start and end apart: 10, of which 8 were waited for; matrix products, arithmetic and copies ran while one was open for 1% of the time, Pallas kernels for 0%

commit v1 on v0

v1 whole, which is shorter than its diff:
```python
import math

import jax
import jax.numpy as jnp
from jax import lax
from jax.experimental import pallas as pl
from jax.experimental.pallas import tpu as pltpu
from jax.sharding import PartitionSpec as P

HEAD = 128
BLOCK = 64
GROUP = 8
DOCS = 16
NBLK = 128
ZH, X, Y, CORE, TP = 2, 4, 4, 2, 4
ROWS = 2 * BLOCK
MINE = ROWS // TP
WIDE = GROUP * HEAD
TILE = 256
PER_TILE = TILE // BLOCK
TILES = 9
LANES = GROUP * BLOCK
SCALE = 1.0 / math.sqrt(HEAD)
SCALE2 = SCALE * math.log2(math.e)
NEGATIVE = -1e30
VMEM_LIMIT = 56 * 1024 * 1024
f32 = jnp.float32
bf16 = jnp.bfloat16


def place():
    c = lax.axis_index("ctx")
    t = lax.axis_index("tp")
    return c // 32, (c // 8) % 4, (c // 2) % 4, c % 2, t


def ctx_of(zh, x, y, core):
    return ((zh * X + x) * Y + y) * CORE + core


def enter(zh, x, y, core, t):
    barrier = pltpu.get_barrier_semaphore()
    me = ctx_of(zh, x, y, core)
    peers = [(me, (t + d) % TP) for d in range(1, TP)]
    peers += [(ctx_of(zh, (x + d) % X, y, core), t) for d in range(1, X)]
    peers += [(ctx_of(zh, x, (y + d) % Y, core), t) for d in range(1, Y)]
    peers += [(ctx_of(1 - zh, x, y, core), t), (ctx_of(zh, x, y, 1 - core), t)]
    for peer in peers:
        pl.semaphore_signal(barrier, inc=1, device_id=peer, device_id_type=pl.DeviceIdType.MESH)
    pl.semaphore_wait(barrier, len(peers))


def remote(src, dst, send, recv, peer):
    return pltpu.make_async_remote_copy(
        src_ref=src,
        dst_ref=dst,
        send_sem=send,
        recv_sem=recv,
        device_id=peer,
        device_id_type=pl.DeviceIdType.MESH,
    )


def columns(index, width):
    return pl.ds(pl.multiple_of(index * width, width), width)


def rows_of(index, count):
    return pl.ds(pl.multiple_of(index * count, count), count)


def gather_kernel(
    q, k, v, g, q_o, g_o, kv_o,
    own_sem, tp_send, tp_recv, wide_send, wide_recv, z_send, z_recv,
    one_send, one_recv, two_send, two_recv, core_send, core_recv,
):
    zh, x, y, core, t = place()
    me = ctx_of(zh, x, y, core)
    enter(zh, x, y, core, t)
    own = kv_o.at[zh, x, y, core]
    sends = []

    small = []
    for d in (2, 1, 3):
        peer = (t + d) % TP
        for i, ref in enumerate((k, v)):
            copy = remote(
                ref.at[:, columns(peer, HEAD)],
                own.at[i, rows_of(t, MINE), :],
                tp_send.at[d - 1, i],
                tp_recv.at[d - 1, i],
                (me, peer),
            )
            copy.start()
            small.append(copy)
    local = []
    for i, ref in enumerate((k, v)):
        copy = pltpu.make_async_copy(
            ref.at[:, columns(t, HEAD)], own.at[i, rows_of(t, MINE), :], own_sem.at[i]
        )
        copy.start()
        local.append(copy)
    for i, (ref, out) in enumerate(((q, q_o), (g, g_o))):
        copy = pltpu.make_async_copy(
            ref.at[:, columns(t, WIDE)], out.at[rows_of(t, MINE), :], own_sem.at[2 + i]
        )
        copy.start()
        local.append(copy)
    for copy in small:
        copy.wait_recv()
    sends += small
    local[0].wait()
    local[1].wait()

    across = remote(own, own, z_send, z_recv, (ctx_of(1 - zh, x, y, core), t))
    across.start()
    across.wait_recv()
    sends.append(across)

    sibling = (ctx_of(zh, x, y, 1 - core), t)

    def x_peer(d):
        return (ctx_of(zh, (x + d) % X, y, core), t)

    def y_peer(d):
        return (ctx_of(zh, x, (y + d) % Y, core), t)

    def chunk(i, dx, dy, which):
        return kv_o.at[:, (x + dx) % X, (y + dy) % Y, which, i]

    firsts = {}
    for d in (2, 1, 3):
        for i in range(2):
            here = chunk(i, 0, 0, core)
            copy = remote(
                here, here, one_send.at[i, d - 1], one_recv.at[i, d - 1],
                x_peer(d) if i == 0 else y_peer(d),
            )
            copy.start()
            firsts[i, d] = copy
            sends.append(copy)

    wide = []
    for i, (ref, out) in enumerate(((q, q_o), (g, g_o))):
        for d in (2, 1, 3):
            peer = (t + d) % TP
            copy = remote(
                ref.at[:, columns(peer, WIDE)],
                out.at[rows_of(t, MINE), :],
                wide_send.at[i, d - 1],
                wide_recv.at[i, d - 1],
                (me, peer),
            )
            copy.start()
            wide.append(copy)
            sends.append(copy)

    seconds = {}
    siblings = []

    def spread(i, d):
        dx, dy = (-d, 0) if i == 0 else (0, -d)
        here = chunk(i, dx, dy, core)
        for e in (2, 1, 3):
            copy = remote(
                here, here, two_send.at[i, d, e - 1], two_recv.at[i, d, e - 1],
                y_peer(e) if i == 0 else x_peer(e),
            )
            copy.start()
            seconds[i, d, e] = copy
            sends.append(copy)
        to_sibling(i, d, 0)

    def to_sibling(i, d, e):
        dx, dy = (-d, -e) if i == 0 else (-e, -d)
        here = chunk(i, dx, dy, core)
        copy = remote(here, here, core_send.at[i, d, e], core_recv.at[i, d, e], sibling)
        copy.start()
        siblings.append(copy)
        sends.append(copy)

    spread(0, 0)
    spread(1, 0)
    for d in (1, 3, 2):
        for i in range(2):
            firsts[i, d].wait_recv()
            spread(i, d)
    for d in (0, 1, 3, 2):
        for e in (1, 3, 2):
            for i in range(2):
                seconds[i, d, e].wait_recv()
                to_sibling(i, d, e)
    for copy in siblings:
        copy.wait_recv()
    for copy in wide:
        copy.wait_recv()
    local[2].wait()
    local[3].wait()
    for copy in sends:
        copy.wait_send()


def gather(queries, keys, values, out_grad):
    dma = pltpu.SemaphoreType.DMA
    return pl.pallas_call(
        gather_kernel,
        out_shape=(
            jax.ShapeDtypeStruct((ROWS, WIDE), bf16),
            jax.ShapeDtypeStruct((ROWS, WIDE), bf16),
            jax.ShapeDtypeStruct((ZH, X, Y, CORE, 2, ROWS, HEAD), bf16),
        ),
        in_specs=[pl.BlockSpec(memory_space=pl.ANY)] * 4,
        out_specs=[pl.BlockSpec(memory_space=pl.ANY)] * 3,
        scratch_shapes=[
            dma((4,)),
            dma((3, 2)), dma((3, 2)),
            dma((2, 3)), dma((2, 3)),
            dma, dma,
            dma((2, 3)), dma((2, 3)),
            dma((2, 4, 3)), dma((2, 4, 3)),
            dma((2, 4, 4)), dma((2, 4, 4)),
        ],
        compiler_params=pltpu.CompilerParams(collective_id=0, has_side_effects=True),
        name="gather",
    )(queries, keys, values, out_grad)


def mm(a, b, ca, cb):
    return lax.dot_general(a, b, (((ca,), (cb,)), ((), ())), preferred_element_type=f32)


def attend_kernel(
    doc, row_block, q_ref, g_ref, kv_ref, att_ref, dq_ref, grad_ref,
    slot_of, s_scr, w_scr, qb, gb, qs, gs,
):
    c = lax.axis_index("ctx")

    def clear(i, carry):
        grad_ref[i] = jnp.zeros(grad_ref.shape[1:], bf16)
        return carry

    lax.fori_loop(0, grad_ref.shape[0], clear, 0)

    def invert(i, carry):
        slot_of[row_block[i]] = i
        return carry

    lax.fori_loop(0, NBLK, invert, 0)
    offset = lax.broadcasted_iota(jnp.int32, (1, LANES), 1) % BLOCK

    for b in range(2):
        block = row_block[2 * c + b]
        first = block * BLOCK
        position = first + offset
        low = jnp.zeros((1, LANES), jnp.int32)
        low_first = jnp.int32(0)
        end = jnp.int32(0)
        for d in range(DOCS):
            end = end + doc[d]
            low = jnp.where(position >= end, end, low)
            low_first = jnp.where(first >= end, end, low_first)
        start = low_first // BLOCK
        tiles = (block - start + PER_TILE) // PER_TILE

        here = pl.ds(b * BLOCK, BLOCK)
        for h in range(GROUP):
            qb[pl.ds(h * BLOCK, BLOCK), :] = q_ref[here, pl.ds(h * HEAD, HEAD)]
            gb[pl.ds(h * BLOCK, BLOCK), :] = g_ref[here, pl.ds(h * HEAD, HEAD)]

        def slots(tile):
            return [
                slot_of[jnp.minimum(start + tile * PER_TILE + i, NBLK - 1)] for i in range(PER_TILE)
            ]

        def load(which, tile):
            return jnp.concatenate([kv_ref[2 * (s // 2) + which, s % 2] for s in slots(tile)], axis=0)

        def scores(tile, top):
            s = mm(load(0, tile), qb[...], 1, 1)
            at = (start + tile * PER_TILE) * BLOCK + lax.broadcasted_iota(
                jnp.int32, (TILE, LANES), 0
            )
            s = jnp.where((at >= low) & (at <= position), s, NEGATIVE)
            s_scr[tile] = s
            return jnp.maximum(top, jnp.max(s.reshape(TILE // 8, 8, LANES), axis=0))

        top8 = lax.fori_loop(0, tiles, scores, jnp.full((8, LANES), NEGATIVE, f32))
        top = jnp.max(top8, axis=0, keepdims=True)

        def weigh(tile, state):
            total8, acc = state
            w = jnp.exp2((s_scr[tile] - top) * SCALE2)
            total8 = total8 + jnp.sum(w.reshape(TILE // 8, 8, LANES), axis=0)
            w16 = w.astype(bf16)
            w_scr[tile] = w16
            return total8, acc + mm(load(1, tile), w16, 0, 0)

        total8, acc = lax.fori_loop(
            0, tiles, weigh, (jnp.zeros((8, LANES), f32), jnp.zeros((HEAD, LANES), f32))
        )
        inv = 1.0 / jnp.sum(total8, axis=0, keepdims=True)
        att_t = acc * inv
        g_t = gb[...].astype(f32).T
        delta = jnp.sum(g_t * att_t, axis=0, keepdims=True)
        att = att_t.T.astype(bf16)
        inv_rows = jnp.broadcast_to(inv, (HEAD, LANES)).T
        gs[...] = (gb[...].astype(f32) * inv_rows).astype(bf16)
        qs[...] = (qb[...].astype(f32) * (inv_rows * SCALE)).astype(bf16)
        for h in range(GROUP):
            att_ref[here, pl.ds(h * HEAD, HEAD)] = att[h * BLOCK : (h + 1) * BLOCK]

        def back(tile, dq_t):
            keys = load(0, tile)
            dp = mm(load(1, tile), gb[...], 1, 1)
            w16 = w_scr[tile]
            ds = (w16.astype(f32) * (dp - delta)).astype(bf16)
            dq_t = dq_t + mm(keys, ds, 0, 0)
            dk = mm(ds, qs[...], 1, 0)
            dv = mm(w16, gs[...], 1, 0)
            for i, s in enumerate(slots(tile)):
                part = slice(i * BLOCK, (i + 1) * BLOCK)
                for which, add in ((0, dk), (1, dv)):
                    old = grad_ref[2 * (s // 2) + which, s % 2]
                    grad_ref[2 * (s // 2) + which, s % 2] = (old.astype(f32) + add[part]).astype(bf16)
            return dq_t

        dq_t = lax.fori_loop(0, tiles, back, jnp.zeros((HEAD, LANES), f32))
        dq = (dq_t * (inv * SCALE)).T.astype(bf16)
        for h in range(GROUP):
            dq_ref[here, pl.ds(h * HEAD, HEAD)] = dq[h * BLOCK : (h + 1) * BLOCK]


def attend(doc_lengths, row_block, q, g, kv):
    vmem = pl.BlockSpec(memory_space=pltpu.VMEM)
    smem = pl.BlockSpec(memory_space=pltpu.SMEM)
    kv = kv.reshape(NBLK, 2, BLOCK, HEAD)
    return pl.pallas_call(
        attend_kernel,
        out_shape=(
            jax.ShapeDtypeStruct((ROWS, WIDE), bf16),
            jax.ShapeDtypeStruct((ROWS, WIDE), bf16),
            jax.ShapeDtypeStruct((NBLK, 2, BLOCK, HEAD), bf16),
        ),
        in_specs=[smem, smem, vmem, vmem, vmem],
        out_specs=[vmem] * 3,
        scratch_shapes=[
            pltpu.SMEM((NBLK,), jnp.int32),
            pltpu.VMEM((TILES, TILE, LANES), f32),
            pltpu.VMEM((TILES, TILE, LANES), bf16),
            pltpu.VMEM((LANES, HEAD), bf16),
            pltpu.VMEM((LANES, HEAD), bf16),
            pltpu.VMEM((LANES, HEAD), bf16),
            pltpu.VMEM((LANES, HEAD), bf16),
        ],
        compiler_params=pltpu.CompilerParams(vmem_limit_bytes=VMEM_LIMIT),
        name="attend",
    )(doc_lengths, row_block, q, g, kv)


def scatter_kernel(
    att, dq, grad, att_o, dq_o, dk_o, dv_o,
    in_core, held, in_one, held_two, in_two, held_z, in_z, final,
    own_sem, wide_send, wide_recv, core_send, core_recv, one_send, one_recv,
    two_send, two_recv, z_send, z_recv, tp_send, tp_recv,
):
    zh, x, y, core, t = place()
    me = ctx_of(zh, x, y, core)
    enter(zh, x, y, core, t)
    sends = []
    sibling = (ctx_of(zh, x, y, 1 - core), t)

    def pieces(i, d, which):
        if i == 0:
            return grad.at[:, (x + d) % X, :, which, i]
        return grad.at[:, :, (y + d) % Y, which, i]

    siblings = {}
    for d in (2, 1, 3, 0):
        for i in range(2):
            copy = remote(
                pieces(i, d, 1 - core), in_core.at[i, d], core_send.at[i, d], core_recv.at[i, d],
                sibling,
            )
            copy.start()
            siblings[i, d] = copy
            sends.append(copy)

    wide, local = [], []
    for i, (ref, out) in enumerate(((att, att_o), (dq, dq_o))):
        for d in (2, 1, 3):
            peer = (t + d) % TP
            copy = remote(
                ref.at[rows_of(peer, MINE), :],
                out.at[:, columns(t, WIDE)],
                wide_send.at[i, d - 1],
                wide_recv.at[i, d - 1],
                (me, peer),
            )
            copy.start()
            wide.append(copy)
            sends.append(copy)
        copy = pltpu.make_async_copy(
            ref.at[rows_of(t, MINE), :], out.at[:, columns(t, WIDE)], own_sem.at[i]
        )
        copy.start()
        local.append(copy)

    def one_peer(i, d):
        if i == 0:
            return (ctx_of(zh, (x + d) % X, y, core), t)
        return (ctx_of(zh, x, (y + d) % Y, core), t)

    firsts = {}
    for d in (2, 1, 3, 0):
        for i in range(2):
            siblings[i, d].wait_recv()

            def add(n, carry):
                a, b = n // 4, n % 4
                if i == 0:
                    mine = grad[a, (x + d) % X, b, core, i]
                else:
                    mine = grad[a, b, (y + d) % Y, core, i]
                held[i, d, a, b] = (mine.astype(f32) + in_core[i, d, a, b].astype(f32)).astype(bf16)
                return carry

            lax.fori_loop(0, 8, add, 0)
            if d > 0:
                copy = remote(
                    held.at[i, d], in_one.at[i, d - 1], one_send.at[i, d - 1],
                    one_recv.at[i, d - 1], one_peer(i, d),
                )
                copy.start()
                firsts[i, d] = copy
                sends.append(copy)

    seconds = {}
    for i in range(2):
        for d in (1, 3, 2):
            firsts[i, d].wait_recv()
        at = y if i == 0 else x
        for e in (2, 1, 3, 0):
            b = (at + e) % 4
            for a in range(2):
                total = held[i, 0, a, b].astype(f32)
                for d in range(3):
                    total = total + in_one[i, d, a, b].astype(f32)
                held_two[i, e, a] = total.astype(bf16)
            if e > 0:
                copy = remote(
                    held_two.at[i, e], in_two.at[i, e - 1], two_send.at[i, e - 1],
                    two_recv.at[i, e - 1], one_peer(1 - i, e),
                )
                copy.start()
                seconds[i, e] = copy
                sends.append(copy)

    across = []
    for i in range(2):
        for e in (1, 3, 2):
            seconds[i, e].wait_recv()
        for a in range(2):
            total = held_two[i, 0, a].astype(f32)
            for e in range(3):
                total = total + in_two[i, e, a].astype(f32)
            held_z[i, a] = total.astype(bf16)
        copy = remote(
            held_z.at[i, 1 - zh], in_z.at[i], z_send.at[i], z_recv.at[i],
            (ctx_of(1 - zh, x, y, core), t),
        )
        copy.start()
        across.append(copy)
        sends.append(copy)

    small = []
    for i, out in enumerate((dk_o, dv_o)):
        across[i].wait_recv()
        final[i] = (held_z[i, zh].astype(f32) + in_z[i].astype(f32)).astype(bf16)
        for d in (2, 1, 3):
            peer = (t + d) % TP
            copy = remote(
                final.at[i, rows_of(peer, MINE), :],
                out.at[:, columns(t, HEAD)],
                tp_send.at[i, d - 1],
                tp_recv.at[i, d - 1],
                (me, peer),
            )
            copy.start()
            small.append(copy)
            sends.append(copy)
        copy = pltpu.make_async_copy(
            final.at[i, rows_of(t, MINE), :], out.at[:, columns(t, HEAD)], own_sem.at[2 + i]
        )
        copy.start()
        local.append(copy)
    for copy in small + wide:
        copy.wait_recv()
    for copy in local:
        copy.wait()
    for copy in sends:
        copy.wait_send()


def scatter(att, dq, grad):
    dma = pltpu.SemaphoreType.DMA
    anywhere = pl.BlockSpec(memory_space=pl.ANY)
    vmem = pl.BlockSpec(memory_space=pltpu.VMEM)
    grad = grad.reshape(ZH, X, Y, CORE, 2, ROWS, HEAD)
    return pl.pallas_call(
        scatter_kernel,
        out_shape=(
            jax.ShapeDtypeStruct((MINE, TP * WIDE), bf16),
            jax.ShapeDtypeStruct((MINE, TP * WIDE), bf16),
            jax.ShapeDtypeStruct((MINE, TP * HEAD), bf16),
            jax.ShapeDtypeStruct((MINE, TP * HEAD), bf16),
        ),
        in_specs=[anywhere, anywhere, vmem],
        out_specs=[anywhere] * 4,
        scratch_shapes=[
            pltpu.VMEM((2, 4, ZH, 4, ROWS, HEAD), bf16),
            pltpu.VMEM((2, 4, ZH, 4, ROWS, HEAD), bf16),
            pltpu.VMEM((2, 3, ZH, 4, ROWS, HEAD), bf16),
            pltpu.VMEM((2, 4, ZH, ROWS, HEAD), bf16),
            pltpu.VMEM((2, 3, ZH, ROWS, HEAD), bf16),
            pltpu.VMEM((2, ZH, ROWS, HEAD), bf16),
            pltpu.VMEM((2, ROWS, HEAD), bf16),
            pltpu.VMEM((2, ROWS, HEAD), bf16),
            dma((4,)),
            dma((2, 3)), dma((2, 3)),
            dma((2, 4)), dma((2, 4)),
            dma((2, 3)), dma((2, 3)),
            dma((2, 3)), dma((2, 3)),
            dma((2,)), dma((2,)),
            dma((2, 3)), dma((2, 3)),
        ],
        compiler_params=pltpu.CompilerParams(
            collective_id=1, has_side_effects=True, vmem_limit_bytes=VMEM_LIMIT
        ),
        name="scatter",
    )(att, dq, grad)


def per_device(queries, keys, values, out_grad, doc_lengths, row_block):
    q, g, kv = gather(queries, keys, values, out_grad)
    att, dq, grad = attend(doc_lengths, row_block, q, g, kv)
    return scatter(att, dq, grad)


def solution(mesh):
    return jax.shard_map(
        per_device,
        mesh=mesh,
        in_specs=(P(("ctx", "tp"), None),) * 4 + (P(), P()),
        out_specs=(P(("ctx", "tp"), None),) * 4,
        check_vma=False,
    )
```

time: 1290 us -> 96.3 us (0.07); the launches traced: 1270 us -> 94.7 us
  waiting for transfers between devices: 952 us -> 0 us
  matrix products: 187 us -> 0 us
  Pallas kernels: 0 us -> 88 us
  local copies, waits for them, and re-layouts: 38.1 us -> 6.09 us
  loops' own time: 22.5 us -> 0 us
  starting transfers between devices: 22.2 us -> 0 us
  other arithmetic: 19.2 us -> 0 us
  blocking collectives: 18.4 us -> 0 us
  between operations: 14 us -> 0.65 us
    reduce_scatter x2 -> x0, waiting for transfers between devices: 794 us -> none  [the longest x1 407 us: per_device(): lax.psum_scatter(value_acc, 'ctx', scatter_dimension=0, tiled=True)]
    dot_general x112 -> x0, matrix products: 187 us -> none  [the longest x16 33.7 us: backward_step(): jnp.einsum('kgts,tkgd->skd', probs.astype(jnp.bfloat16), g_four, preferre...]
    all_gather x2 -> x0, waiting for transfers between devices: 137 us -> none  [the longest x1 80.4 us: per_device(): lax.all_gather(v_local, 'ctx', axis=0, tiled=True)]
    pallas_call x0 -> x3, Pallas kernels: none -> 88 us  [the longest x1 38.2 us: gather(): pl.pallas_call(gather_kernel, out_shape=(jax.ShapeDtypeStruct((ROWS, WIDE...]
    dynamic_slice x98 -> x0, local copies, waits for them, and re-layouts: 23.7 us -> none  [the longest x32 18.7 us: over_blocks(): lax.scan(inner, carry, (jnp.arange(pieces, dtype=jnp.int32), key_split, v...]
    another operation x2 -> x0, loops' own time: 22.5 us -> none  [over_blocks(): lax.scan(inner, carry, (jnp.arange(pieces, dtype=jnp.int32), key_split, v...]
    all_to_all x6 -> x0, starting transfers between devices: 22 us -> none  [the longest x1 4.19 us: per_device(): lax.all_to_all(key_mine.astype(jnp.bfloat16), 'tp', split_axis=0, concat_...]
    all_to_all x6 -> x0, waiting for transfers between devices: 20.4 us -> none  [the longest x1 7.52 us: per_device(): lax.all_to_all(attended_rows, 'tp', split_axis=0, concat_axis=1, tiled=True)]
  transfers between devices with their start and end apart: 10 -> 0, of which waited for: 8 -> 0; matrix products, arithmetic and copies ran while one was open for 1% -> 0% of each run, Pallas kernels for 0% -> 0%
where the time goes in v1:
time: 96.3 us; the launch traced here: 94.7 us
  Pallas kernels  88 us (91%)
  local copies, waits for them, and re-layouts  6.09 us (6%)
    pallas_call x1, Pallas kernels, gather(): pl.pallas_call(gather_kernel, out_shape=(jax.ShapeDtypeStruct((ROWS, WIDE...  38.2 us
    pallas_call x1, Pallas kernels, scatter(): pl.pallas_call(scatter_kernel, out_shape=(jax.ShapeDtypeStruct((MINE, TP...  32 us
    pallas_call x1, Pallas kernels, attend(): pl.pallas_call(attend_kernel, out_shape=(jax.ShapeDtypeStruct((ROWS, WIDE...  17.8 us
    unnamed x4, local copies, waits for them, and re-layouts  6.09 us

profile of v1, /device:TPU:1, one launch (start us, length us, event | category | flops | bytes accessed | tf_op | source)
XLA Modules:
  0.0 94.7 jit_solution(3024652946199358687)
XLA Ops:
  0.6 38.2 %gather.1 = (bf16[128,1024]{1,0:T(8,128)(2,1)}, bf16[128,1024]{1,0:T(8,128)(2,1)}, bf16[2,4,4,2,2,128,128]{6,5,4,3,2,1,0:T(8,128)(2,1)}) custom-call(bf16[32,4096]{1,0:T(8,128)(2,1)} %q.1, bf16[32,512]{1,0:T(8,128)(2,1)} %k.1, bf16[32,512]{1,0:T(8,128)(2,1)} %v.1, bf16[32,4096]{1,0:T(8,128)(2,1)} %g.1), custom_call_target="tpu_custom_call" | custom-call | tf_op jit(solution)/shard_map/gather/pallas_call | solution.py:205
  38.9 17.8 %attend.1 = (bf16[128,1024]{1,0:T(8,128)(2,1)}, bf16[128,1024]{1,0:T(8,128)(2,1)}, bf16[128,2,64,128]{3,2,1,0:T(8,128)(2,1)}) custom-call(s32[16]{0:T(128)} %doc.1, s32[128]{0:T(128)} %row_block.1, bf16[128,1024]{1,0:T(8,128)(2,1)} %get-tuple-element.10.q_ref, bf16[128,1024]{1,0:T(8,128)(2,1)} %get-tuple-element.11.g_ref, bf16[128,2,64,128]{3,2,1,0:T(8,128)(2,1)} %bitcast.2), custom_call_target="tpu_custom_call" | custom-call | tf_op jit(solution)/shard_map/attend/pallas_call | solution.py:337
  56.6 32.0 %scatter.1 = (bf16[32,4096]{1,0:T(8,128)(2,1)}, bf16[32,4096]{1,0:T(8,128)(2,1)}, bf16[32,512]{1,0:T(8,128)(2,1)}, bf16[32,512]{1,0:T(8,128)(2,1)}) custom-call(bf16[128,1024]{1,0:T(8,128)(2,1)} %get-tuple-element.13.att, bf16[128,1024]{1,0:T(8,128)(2,1)} %get-tuple-element.14.dq, bf16[2,4,4,2,2,128,128]{6,5,4,3,2,1,0:T(8,128)(2,1)} %bitcast.3), custom_call_target="tpu_custom_call" | custom-call | tf_op jit(solution)/shard_map/scatter/pallas_call | solution.py:509
  88.6 1.7 %copy.14 = bf16[32,4096]{1,0:T(8,128)(2,1)} copy(bf16[32,4096]{1,0:T(8,128)(2,1)} %get-tuple-element.20) | data formatting | bytes 524288
  90.3 1.7 %copy.15 = bf16[32,4096]{1,0:T(8,128)(2,1)} copy(bf16[32,4096]{1,0:T(8,128)(2,1)} %get-tuple-element.21) | data formatting | bytes 524288
  91.9 1.4 %copy.16 = bf16[32,512]{1,0:T(8,128)(2,1)} copy(bf16[32,512]{1,0:T(8,128)(2,1)} %get-tuple-element.22) | data formatting | bytes 65536
  93.3 1.4 %copy.17 = bf16[32,512]{1,0:T(8,128)(2,1)} copy(bf16[32,512]{1,0:T(8,128)(2,1)} %get-tuple-element.23) | data formatting | bytes 65536

commit v2 on v0

v2 whole, which is shorter than its diff:
```python
import math

import jax
import jax.numpy as jnp
from jax import lax
from jax.experimental import pallas as pl
from jax.experimental.pallas import tpu as pltpu
from jax.sharding import PartitionSpec as P

HEAD = 128
BLOCK = 64
GROUP = 8
DOCS = 16
NBLK = 128
ZH, X, Y, CORE, TP = 2, 4, 4, 2, 4
ROWS = 2 * BLOCK
MINE = ROWS // TP
WIDE = GROUP * HEAD
TILE = 256
BACK = 2048 // BLOCK
WINDOW = (BACK + 1) * BLOCK
TILES = BACK * BLOCK // TILE
LANES = GROUP * BLOCK
SCALE = 1.0 / math.sqrt(HEAD)
SCALE2 = SCALE * math.log2(math.e)
NEGATIVE = -1e30
VMEM_LIMIT = 56 * 1024 * 1024
f32 = jnp.float32
bf16 = jnp.bfloat16


def place():
    c = lax.axis_index("ctx")
    t = lax.axis_index("tp")
    return c // 32, (c // 8) % 4, (c // 2) % 4, c % 2, t


def ctx_of(zh, x, y, core):
    return ((zh * X + x) * Y + y) * CORE + core


def enter(me, t, zh, x, y, core):
    barrier = pltpu.get_barrier_semaphore()
    peers = near(zh, x, y, core, t)
    peers += [(ctx_of(zh, (x + d) % X, y, core), t) for d in range(1, X)]
    peers += [(ctx_of(zh, x, (y + d) % Y, core), t) for d in range(1, Y)]
    peers += [(ctx_of(zh, x, y, 1 - core), t)]
    for peer in peers:
        pl.semaphore_signal(barrier, inc=1, device_id=peer, device_id_type=pl.DeviceIdType.MESH)
    pl.semaphore_wait(barrier, len(peers))


def near(zh, x, y, core, t):
    return [
        (ctx_of((zh + a) % ZH, x, y, core), (t + d) % TP)
        for a in range(ZH)
        for d in range(TP)
        if a + d > 0
    ]


def remote(src, dst, send, recv, peer):
    return pltpu.make_async_remote_copy(
        src_ref=src,
        dst_ref=dst,
        send_sem=send,
        recv_sem=recv,
        device_id=peer,
        device_id_type=pl.DeviceIdType.MESH,
    )


def columns(index, width):
    return pl.ds(pl.multiple_of(index * width, width), width)


def rows_of(index, count):
    return pl.ds(pl.multiple_of(index * count, count), count)


def mm(a, b, ca, cb):
    return lax.dot_general(a, b, (((ca,), (cb,)), ((), ())), preferred_element_type=f32)


def fused_kernel(
    doc, row_block, slot_of, q, k, v, g, att_o, dq_o, dk_o, dv_o,
    kbuf, vbuf, q_in, g_in, kwin, vwin, qh, gh, qs, gs, s_scr, w_scr, dk_rel, dv_rel,
    out_core, in_core, held, in_one, held_two, in_two, held_z, in_fin,
    own_sem, tp_send, tp_recv, wide_send, wide_recv, one_send, one_recv, two_send, two_recv,
    core_send, core_recv, res_send, res_recv, r0_send, r0_recv, r1_send, r1_recv,
    r2_send, r2_recv, r3_send, r3_recv,
):
    zh, x, y, core, t = place()
    c = lax.axis_index("ctx")
    enter(c, t, zh, x, y, core)
    peers = near(zh, x, y, core, t)
    sibling = (ctx_of(zh, x, y, 1 - core), t)
    sends = []

    def go(copy):
        copy.start()
        sends.append(copy)
        return copy

    def x_peer(d):
        return (ctx_of(zh, (x + d) % X, y, core), t)

    def y_peer(d):
        return (ctx_of(zh, x, (y + d) % Y, core), t)

    bufs = (kbuf, vbuf)

    mine = pl.ds(pl.multiple_of((t % 2) * MINE, MINE), MINE)
    small = []
    for n, peer in enumerate(peers):
        for i, ref in enumerate((k, v)):
            small.append(go(remote(
                ref.at[:, columns(peer[1], HEAD)],
                bufs[i].at[zh, x, y, core, t // 2, mine, :],
                tp_send.at[n, i], tp_recv.at[n, i], peer,
            )))
    local = []
    for i, ref in enumerate((k, v)):
        local.append(pltpu.make_async_copy(
            ref.at[:, columns(t, HEAD)], bufs[i].at[zh, x, y, core, t // 2, mine, :], own_sem.at[i]
        ))
    for i, (ref, to) in enumerate(((q, q_in), (g, g_in))):
        local.append(pltpu.make_async_copy(
            ref.at[:, columns(t, WIDE)], to.at[rows_of(t, MINE), :], own_sem.at[2 + i]
        ))
    for copy in local:
        copy.start()

    for copy in small:
        copy.wait_recv()
    local[0].wait()
    local[1].wait()

    def chunk(i, dx, dy):
        return bufs[i].at[:, (x + dx) % X, (y + dy) % Y, core]

    firsts = {}
    for d in (2, 1, 3):
        for i in range(2):
            here = chunk(i, 0, 0)
            firsts[i, d] = go(remote(
                here, here, one_send.at[i, d - 1], one_recv.at[i, d - 1],
                x_peer(d) if i == 0 else y_peer(d),
            ))

    wide = []
    for i, (ref, to) in enumerate(((q, q_in), (g, g_in))):
        for d in (2, 1, 3):
            peer = (t + d) % TP
            wide.append(go(remote(
                ref.at[:, columns(peer, WIDE)], to.at[rows_of(t, MINE), :],
                wide_send.at[i, d - 1], wide_recv.at[i, d - 1], (c, peer),
            )))

    seconds = {}
    siblings = []

    def to_sibling(i, d, e):
        dx, dy = (-d, -e) if i == 0 else (-e, -d)
        here = chunk(i, dx, dy)
        siblings.append(go(remote(
            here, here, core_send.at[i, d, e], core_recv.at[i, d, e], sibling
        )))

    def spread(i, d):
        dx, dy = (-d, 0) if i == 0 else (0, -d)
        here = chunk(i, dx, dy)
        for e in (2, 1, 3):
            seconds[i, d, e] = go(remote(
                here, here, two_send.at[i, d, e - 1], two_recv.at[i, d, e - 1],
                y_peer(e) if i == 0 else x_peer(e),
            ))
        to_sibling(i, d, 0)

    spread(0, 0)
    spread(1, 0)
    for d in (1, 3, 2):
        for i in range(2):
            firsts[i, d].wait_recv()
            spread(i, d)
    for d in (0, 1, 3, 2):
        for e in (1, 3, 2):
            for i in range(2):
                seconds[i, d, e].wait_recv()
                to_sibling(i, d, e)

    for copy in wide:
        copy.wait_recv()
    local[2].wait()
    local[3].wait()
    for b in range(2):
        here = pl.ds(b * BLOCK, BLOCK)
        for h in range(GROUP):
            qh[b, pl.ds(h * BLOCK, BLOCK), :] = q_in[here, pl.ds(h * HEAD, HEAD)]
            gh[b, pl.ds(h * BLOCK, BLOCK), :] = g_in[here, pl.ds(h * HEAD, HEAD)]

    offset = lax.broadcasted_iota(jnp.int32, (1, LANES), 1) % BLOCK
    base, low = [], []
    for b in range(2):
        block = row_block[2 * c + b]
        position = block * BLOCK + offset
        lowest = jnp.zeros((1, LANES), jnp.int32)
        end = jnp.int32(0)
        for d in range(DOCS):
            end = end + doc[d]
            lowest = jnp.where(position >= end, end, lowest)
        base.append(block - BACK)
        low.append(lowest - (block - BACK) * BLOCK)

    for copy in siblings:
        copy.wait_recv()

    def window(j, carry):
        to = pl.ds(pl.multiple_of(j * BLOCK, BLOCK), BLOCK)
        for b in range(2):
            s = slot_of[jnp.maximum(base[b] + j, 0)]
            at = tuple(lax.rem(lax.div(s, n), m) for n, m in ((64, 2), (16, 4), (4, 4), (2, 2), (1, 2)))
            kwin[b, to, :] = kbuf[at]
            vwin[b, to, :] = vbuf[at]
        return carry

    lax.fori_loop(0, BACK + 1, window, 0)

    def keys_of(tile):
        return pl.ds(pl.multiple_of(tile * TILE, TILE), TILE)

    tail = pl.ds(BACK * BLOCK, BLOCK)
    at_tile = lax.broadcasted_iota(jnp.int32, (TILE, LANES), 0)
    at_tail = lax.broadcasted_iota(jnp.int32, (BLOCK, LANES), 0)

    def folded(values, fold):
        return fold(values.reshape(values.shape[0] // 8, 8, LANES), axis=0)

    def scores(tile, tops):
        out = []
        for b in range(2):
            s = mm(kwin[b, keys_of(tile), :], qh[b], 1, 1)
            s = jnp.where(at_tile >= low[b] - tile * TILE, s, NEGATIVE)
            s_scr[b, keys_of(tile), :] = s
            out.append(jnp.maximum(tops[b], folded(s, jnp.max)))
        return tuple(out)

    tops = []
    for b in range(2):
        s = mm(kwin[b, tail, :], qh[b], 1, 1)
        seen = (at_tail >= low[b] - BACK * BLOCK) & (at_tail <= offset)
        s = jnp.where(seen, s, NEGATIVE)
        s_scr[b, tail, :] = s
        tops.append(folded(s, jnp.max))
    tops = lax.fori_loop(0, TILES, scores, tuple(tops))
    tops = [jnp.max(top, axis=0, keepdims=True) for top in tops]

    def weigh_part(b, part, total, acc):
        w = jnp.exp2((s_scr[b, part, :] - tops[b]) * SCALE2)
        total = total + folded(w, jnp.sum)
        w16 = w.astype(bf16)
        w_scr[b, part, :] = w16
        return total, acc + mm(vwin[b, part, :], w16, 0, 0)

    def weigh(tile, state):
        out = [weigh_part(b, keys_of(tile), *state[b]) for b in range(2)]
        return tuple(out)

    state = tuple(
        weigh_part(b, tail, jnp.zeros((8, LANES), f32), jnp.zeros((HEAD, LANES), f32))
        for b in range(2)
    )
    state = lax.fori_loop(0, TILES, weigh, state)

    inverse, delta = [], []
    results = []

    for b in range(2):
        total, acc = state[b]
        inv = 1.0 / jnp.sum(total, axis=0, keepdims=True)
        att_t = acc * inv
        g_t = gh[b].astype(f32).T
        delta.append(jnp.sum(g_t * att_t, axis=0, keepdims=True))
        inverse.append(inv)
        att = att_t.T.astype(bf16)
        inv_rows = jnp.broadcast_to(inv, (HEAD, LANES)).T
        gs[b] = (gh[b].astype(f32) * inv_rows).astype(bf16)
        qs[b] = (qh[b].astype(f32) * (inv_rows * SCALE)).astype(bf16)
        for h in range(GROUP):
            q_in[pl.ds(b * BLOCK, BLOCK), pl.ds(h * HEAD, HEAD)] = att[h * BLOCK : (h + 1) * BLOCK]

    def send_rows(i, ref, out):
        for d in (2, 1, 3):
            peer = (t + d) % TP
            results.append(go(remote(
                ref.at[rows_of(peer, MINE), :], out.at[:, columns(t, WIDE)],
                res_send.at[i, d - 1], res_recv.at[i, d - 1], (c, peer),
            )))
        copy = pltpu.make_async_copy(
            ref.at[rows_of(t, MINE), :], out.at[:, columns(t, WIDE)], own_sem.at[5 + i]
        )
        copy.start()
        local.append(copy)

    send_rows(0, q_in, att_o)

    def back_part(b, part, first, dq_t):
        keys = kwin[b, part, :]
        dp = mm(vwin[b, part, :], gh[b], 1, 1)
        w16 = w_scr[b, part, :]
        ds = (w16.astype(f32) * (dp - delta[b])).astype(bf16)
        to = pl.ds(first + 1, w16.shape[0] // BLOCK)
        dk_rel[b, to] = mm(ds, qs[b], 1, 0).reshape(-1, BLOCK, HEAD)
        dv_rel[b, to] = mm(w16, gs[b], 1, 0).reshape(-1, BLOCK, HEAD)
        return dq_t + mm(keys, ds, 0, 0)

    def back(tile, state):
        return tuple(back_part(b, keys_of(tile), tile * (TILE // BLOCK), state[b]) for b in range(2))

    dqs = tuple(back_part(b, tail, BACK, jnp.zeros((HEAD, LANES), f32)) for b in range(2))
    dqs = lax.fori_loop(0, TILES, back, dqs)
    for b in range(2):
        dq = (dqs[b] * (inverse[b] * SCALE)).T.astype(bf16)
        for h in range(GROUP):
            g_in[pl.ds(b * BLOCK, BLOCK), pl.ds(h * HEAD, HEAD)] = dq[h * BLOCK : (h + 1) * BLOCK]

    rels = (dk_rel, dv_rel)
    for ref in rels:
        for b in range(2):
            for zero in (0, BACK + 2):
                ref[b, zero] = jnp.zeros((BLOCK, HEAD), f32)

    def piece(i, d, e, a, which, half):
        dx, dy = (d, e) if i == 0 else (e, d)
        s = ctx_of(a, (x + dx) % X, (y + dy) % Y, which) * 2 + half
        total = None
        for b in range(2):
            rel = row_block[s] - base[b] + 1
            part = rels[i][b, jnp.minimum(jnp.maximum(rel, 0), BACK + 2)]
            total = part if total is None else total + part
        return total

    def one_peer(i, d):
        return x_peer(d) if i == 0 else y_peer(d)

    order = [(d, i) for d in (2, 1, 3, 0) for i in range(2)]
    r0 = {}
    for d, i in order:
        def assemble(e, carry):
            for a in range(ZH):
                for half in range(2):
                    out_core[i, d, e, a, half] = piece(i, d, e, a, 1 - core, half).astype(bf16)
            return carry

        lax.fori_loop(0, 4, assemble, 0)
        r0[i, d] = go(remote(
            out_core.at[i, d], in_core.at[i, d], r0_send.at[i, d], r0_recv.at[i, d], sibling
        ))
    send_rows(1, g_in, dq_o)

    def r1(i, d, e):
        return remote(
            held.at[i, d, e], in_one.at[i, d - 1, e], r1_send.at[i, d - 1, e],
            r1_recv.at[i, d - 1, e], one_peer(i, d),
        )

    for d, i in order:
        r0[i, d].wait_recv()

        def add(n, carry):
            e = (n + 1) % 4
            for a in range(ZH):
                for half in range(2):
                    total = piece(i, d, e, a, core, half) + in_core[i, d, e, a, half].astype(f32)
                    held[i, d, e, a, half] = total.astype(bf16)
            if d > 0:
                r1(i, d, e).start()
            return carry

        lax.fori_loop(0, 4, add, 0)

    def r2(i, e):
        return remote(
            held_two.at[i, e], in_two.at[i, e - 1], r2_send.at[i, e - 1], r2_recv.at[i, e - 1],
            one_peer(1 - i, e),
        )

    for e in (1, 2, 3, 0):
        for i in range(2):
            for d in (1, 3, 2):
                r1(i, d, e).wait_recv()
            for a in range(ZH):
                total = held[i, 0, e, a].astype(f32)
                for d in range(3):
                    total = total + in_one[i, d, e, a].astype(f32)
                held_two[i, e, a] = total.astype(bf16)
            if e > 0:
                go(r2(i, e))

    last = []
    for i in range(2):
        for e in (1, 2, 3):
            r2(i, e).wait_recv()
        for a in range(ZH):
            total = held_two[i, 0, a].astype(f32)
            for e in range(3):
                total = total + in_two[i, e, a].astype(f32)
            held_z[i, a] = total.astype(bf16)
        for n, peer in enumerate(peers):
            a = (zh + (n + 1) // TP) % ZH
            last.append(go(remote(
                held_z.at[i, a, peer[1] // 2, pl.ds(pl.multiple_of((peer[1] % 2) * MINE, MINE), MINE), :],
                in_fin.at[i, zh, t], r3_send.at[i, n], r3_recv.at[i, n], peer,
            )))
        in_fin[i, zh, t] = held_z[i, zh, t // 2, mine, :]
    for i, out in enumerate((dk_o, dv_o)):
        for n in range(len(peers)):
            last[i * len(peers) + n].wait_recv()
        for h in range(TP):
            total = in_fin[i, 0, h].astype(f32) + in_fin[i, 1, h].astype(f32)
            out[:, pl.ds(h * HEAD, HEAD)] = total.astype(bf16)
    for copy in results:
        copy.wait_recv()
    for copy in local[4:]:
        copy.wait()
    for copy in sends:
        copy.wait_send()
    for i in range(2):
        for d in range(1, 4):
            for e in range(4):
                r1(i, d, e).wait_send()


def fused(doc_lengths, row_block, queries, keys, values, out_grad):
    dma = pltpu.SemaphoreType.DMA
    anywhere = pl.BlockSpec(memory_space=pl.ANY)
    vmem = pl.BlockSpec(memory_space=pltpu.VMEM)
    smem = pl.BlockSpec(memory_space=pltpu.SMEM)
    V = pltpu.VMEM
    slots = (ZH, X, Y, CORE, 2, BLOCK, HEAD)
    piece = (2, BLOCK, HEAD)
    number = jnp.arange(NBLK, dtype=jnp.int32)
    found = row_block[None, :] == number[:, None]
    slot_of = jnp.sum(jnp.where(found, number[None, :], 0), axis=1)
    return pl.pallas_call(
        fused_kernel,
        out_shape=(
            jax.ShapeDtypeStruct((MINE, TP * WIDE), bf16),
            jax.ShapeDtypeStruct((MINE, TP * WIDE), bf16),
            jax.ShapeDtypeStruct((MINE, TP * HEAD), bf16),
            jax.ShapeDtypeStruct((MINE, TP * HEAD), bf16),
        ),
        in_specs=[smem, smem, smem] + [anywhere] * 4,
        out_specs=[anywhere] * 2 + [vmem] * 2,
        scratch_shapes=[
            V(slots, bf16), V(slots, bf16),
            V((ROWS, WIDE), bf16), V((ROWS, WIDE), bf16),
            V((2, WINDOW, HEAD), bf16), V((2, WINDOW, HEAD), bf16),
            V((2, LANES, HEAD), bf16), V((2, LANES, HEAD), bf16),
            V((2, LANES, HEAD), bf16), V((2, LANES, HEAD), bf16),
            V((2, WINDOW, LANES), f32), V((2, WINDOW, LANES), bf16),
            V((2, BACK + 3, BLOCK, HEAD), f32), V((2, BACK + 3, BLOCK, HEAD), f32),
            V((2, 4, 4, ZH) + piece, bf16), V((2, 4, 4, ZH) + piece, bf16),
            V((2, 4, 4, ZH) + piece, bf16), V((2, 3, 4, ZH) + piece, bf16),
            V((2, 4, ZH) + piece, bf16), V((2, 3, ZH) + piece, bf16),
            V((2, ZH) + piece, bf16), V((2, ZH, TP, MINE, HEAD), bf16),
            dma((7,)),
            dma((7, 2)), dma((7, 2)),
            dma((2, 3)), dma((2, 3)),
            dma((2, 3)), dma((2, 3)),
            dma((2, 4, 3)), dma((2, 4, 3)),
            dma((2, 4, 4)), dma((2, 4, 4)),
            dma((2, 3)), dma((2, 3)),
            dma((2, 4)), dma((2, 4)),
            dma((2, 3, 4)), dma((2, 3, 4)),
            dma((2, 3)), dma((2, 3)),
            dma((2, 7)), dma((2, 7)),
        ],
        compiler_params=pltpu.CompilerParams(
            collective_id=0, has_side_effects=True, vmem_limit_bytes=VMEM_LIMIT
        ),
        name="fused",
    )(doc_lengths, row_block, slot_of, queries, keys, values, out_grad)


def hand_over_kernel(*refs):
    held, sems = refs[8:12], refs[12]
    arrive = [pltpu.make_async_copy(refs[i], held[i], sems.at[0, i]) for i in range(4)]
    leave = [pltpu.make_async_copy(held[i], refs[4 + i], sems.at[1, i]) for i in range(4)]
    for copy in arrive:
        copy.start()
    for i in range(4):
        arrive[i].wait()
        leave[i].start()
    for copy in leave:
        copy.wait()


def hand_over(arrays):
    anywhere = pl.BlockSpec(memory_space=pl.ANY)
    return pl.pallas_call(
        hand_over_kernel,
        out_shape=tuple(jax.ShapeDtypeStruct(a.shape, a.dtype) for a in arrays),
        in_specs=[anywhere] * 4,
        out_specs=[anywhere] * 4,
        scratch_shapes=[pltpu.VMEM(a.shape, a.dtype) for a in arrays]
        + [pltpu.SemaphoreType.DMA((2, 4))],
        name="hand_over",
    )(*arrays)


def per_device(queries, keys, values, out_grad, doc_lengths, row_block):
    return hand_over(fused(doc_lengths, row_block, queries, keys, values, out_grad))


def solution(mesh):
    return jax.shard_map(
        per_device,
        mesh=mesh,
        in_specs=(P(("ctx", "tp"), None),) * 4 + (P(), P()),
        out_specs=(P(("ctx", "tp"), None),) * 4,
        check_vma=False,
    )
```

time: 1290 us -> 79.5 us (0.06); the launches traced: 1270 us -> 79.3 us
  waiting for transfers between devices: 952 us -> 0 us
  matrix products: 187 us -> 0 us
  Pallas kernels: 0 us -> 77.4 us
  local copies, waits for them, and re-layouts: 38.1 us -> 0 us
  loops' own time: 22.5 us -> 0 us
  starting transfers between devices: 22.2 us -> 0 us
  blocking collectives: 18.4 us -> 0 us
  other arithmetic: 19.2 us -> 1.28 us
  between operations: 14 us -> 0.64 us
    reduce_scatter x2 -> x0, waiting for transfers between devices: 794 us -> none  [the longest x1 407 us: per_device(): lax.psum_scatter(value_acc, 'ctx', scatter_dimension=0, tiled=True)]
    dot_general x112 -> x0, matrix products: 187 us -> none  [the longest x16 33.7 us: backward_step(): jnp.einsum('kgts,tkgd->skd', probs.astype(jnp.bfloat16), g_four, preferre...]
    all_gather x2 -> x0, waiting for transfers between devices: 137 us -> none  [the longest x1 80.4 us: per_device(): lax.all_gather(v_local, 'ctx', axis=0, tiled=True)]
    pallas_call x0 -> x2, Pallas kernels: none -> 77.4 us  [the longest x1 75.6 us: fused(): pl.pallas_call(fused_kernel, out_shape=(jax.ShapeDtypeStruct((MINE, TP *...]
    dynamic_slice x98 -> x0, local copies, waits for them, and re-layouts: 23.7 us -> none  [the longest x32 18.7 us: over_blocks(): lax.scan(inner, carry, (jnp.arange(pieces, dtype=jnp.int32), key_split, v...]
    another operation x2 -> x0, loops' own time: 22.5 us -> none  [over_blocks(): lax.scan(inner, carry, (jnp.arange(pieces, dtype=jnp.int32), key_split, v...]
    all_to_all x6 -> x0, starting transfers between devices: 22 us -> none  [the longest x1 4.19 us: per_device(): lax.all_to_all(key_mine.astype(jnp.bfloat16), 'tp', split_axis=0, concat_...]
    all_to_all x6 -> x0, waiting for transfers between devices: 20.4 us -> none  [the longest x1 7.52 us: per_device(): lax.all_to_all(attended_rows, 'tp', split_axis=0, concat_axis=1, tiled=True)]
  transfers between devices with their start and end apart: 10 -> 0, of which waited for: 8 -> 0; matrix products, arithmetic and copies ran while one was open for 1% -> 0% of each run, Pallas kernels for 0% -> 0%
where the time goes in v2:
time: 79.5 us; the launch traced here: 79.3 us
  Pallas kernels  77.4 us (97%)
  other arithmetic  1.28 us (2%)
    pallas_call x1, Pallas kernels, fused(): pl.pallas_call(fused_kernel, out_shape=(jax.ShapeDtypeStruct((MINE, TP *...  75.6 us
    pallas_call x1, Pallas kernels, hand_over(): pl.pallas_call(hand_over_kernel, out_shape=tuple((jax.ShapeDtypeStruct(a....  1.82 us

profile of v2, /device:TPU:1, one launch (start us, length us, event | category | flops | bytes accessed | tf_op | source)
XLA Modules:
  0.0 79.3 jit_solution(1340340459239656684)
XLA Ops:
  0.6 1.3 %select_reduce_fusion.slot_of = s32[128]{0:T(128)} fusion(s32[128]{0:T(128)} %row_block.1), kind=kLoop, calls=%fused_computation | loop fusion | flops 49024 | bytes 1024 | tf_op jit(solution)/shard_map/reduce_sum | solution.py:444
  1.9 75.6 %fused.1 = (bf16[32,4096]{1,0:T(8,128)(2,1)}, bf16[32,4096]{1,0:T(8,128)(2,1)}, bf16[32,512]{1,0:T(8,128)(2,1)}, bf16[32,512]{1,0:T(8,128)(2,1)}) custom-call(s32[16]{0:T(128)} %doc.1, s32[128]{0:T(128)} %row_block.1, s32[128]{0:T(128)} %select_reduce_fusion.slot_of, bf16[32,4096]{1,0:T(8,128)(2,1)} %q.1, bf16[32,512]{1,0:T(8,128)(2,1)} %k.1, ...), custom_call_target="tpu_custom_call" | custom-call | tf_op jit(solution)/shard_map/fused/pallas_call | solution.py:445
  77.5 1.8 %hand_over.1 = (bf16[32,4096]{1,0:T(8,128)(2,1)}, bf16[32,4096]{1,0:T(8,128)(2,1)}, bf16[32,512]{1,0:T(8,128)(2,1)}, bf16[32,512]{1,0:T(8,128)(2,1)}) custom-call(bf16[32,4096]{1,0:T(8,128)(2,1)} %get-tuple-element.8.refs_0_, bf16[32,4096]{1,0:T(8,128)(2,1)} %get-tuple-element.9.refs_1_, bf16[32,512]{1,0:T(8,128)(2,1)} %get-tuple-element.10.refs_2_, ...), custom_call_target="tpu_custom_call" | custom-call | tf_op jit(solution)/shard_map/hand_over/pallas_call | solution.py:501

commit v3 on v2

--- a/solution.py
+++ b/solution.py
@@ -16,7 +16,7 @@
 ROWS = 2 * BLOCK
 MINE = ROWS // TP
 WIDE = GROUP * HEAD
-TILE = 256
+TILE = 512
 BACK = 2048 // BLOCK
 WINDOW = (BACK + 1) * BLOCK
 TILES = BACK * BLOCK // TILE
@@ -252,7 +252,7 @@
         s = jnp.where(seen, s, NEGATIVE)
         s_scr[b, tail, :] = s
         tops.append(folded(s, jnp.max))
-    tops = lax.fori_loop(0, TILES, scores, tuple(tops))
+    tops = lax.fori_loop(0, TILES, scores, tuple(tops), unroll=TILES)
     tops = [jnp.max(top, axis=0, keepdims=True) for top in tops]
 
     def weigh_part(b, part, total, acc):
@@ -270,7 +270,7 @@
         weigh_part(b, tail, jnp.zeros((8, LANES), f32), jnp.zeros((HEAD, LANES), f32))
         for b in range(2)
     )
-    state = lax.fori_loop(0, TILES, weigh, state)
+    state = lax.fori_loop(0, TILES, weigh, state, unroll=TILES)
 
     inverse, delta = [], []
     results = []
@@ -304,25 +304,18 @@
 
     send_rows(0, q_in, att_o)
 
-    def back_part(b, part, first, dq_t):
-        keys = kwin[b, part, :]
-        dp = mm(vwin[b, part, :], gh[b], 1, 1)
-        w16 = w_scr[b, part, :]
-        ds = (w16.astype(f32) * (dp - delta[b])).astype(bf16)
-        to = pl.ds(first + 1, w16.shape[0] // BLOCK)
-        dk_rel[b, to] = mm(ds, qs[b], 1, 0).reshape(-1, BLOCK, HEAD)
-        dv_rel[b, to] = mm(w16, gs[b], 1, 0).reshape(-1, BLOCK, HEAD)
-        return dq_t + mm(keys, ds, 0, 0)
-
-    def back(tile, state):
-        return tuple(back_part(b, keys_of(tile), tile * (TILE // BLOCK), state[b]) for b in range(2))
-
-    dqs = tuple(back_part(b, tail, BACK, jnp.zeros((HEAD, LANES), f32)) for b in range(2))
-    dqs = lax.fori_loop(0, TILES, back, dqs)
+    def value_part(b, part, first):
+        dv = mm(w_scr[b, part, :], gs[b], 1, 0)
+        dv_rel[b, pl.ds(first + 1, dv.shape[0] // BLOCK)] = dv.reshape(-1, BLOCK, HEAD)
+
+    def value_tile(tile, carry):
+        for b in range(2):
+            value_part(b, keys_of(tile), tile * (TILE // BLOCK))
+        return carry
+
     for b in range(2):
-        dq = (dqs[b] * (inverse[b] * SCALE)).T.astype(bf16)
-        for h in range(GROUP):
-            g_in[pl.ds(b * BLOCK, BLOCK), pl.ds(h * HEAD, HEAD)] = dq[h * BLOCK : (h + 1) * BLOCK]
+        value_part(b, tail, BACK)
+    lax.fori_loop(0, TILES, value_tile, 0, unroll=TILES)
 
     rels = (dk_rel, dv_rel)
     for ref in rels:
@@ -330,9 +323,9 @@
             for zero in (0, BACK + 2):
                 ref[b, zero] = jnp.zeros((BLOCK, HEAD), f32)
 
-    def piece(i, d, e, a, which, half):
-        dx, dy = (d, e) if i == 0 else (e, d)
-        s = ctx_of(a, (x + dx) % X, (y + dy) % Y, which) * 2 + half
+    def piece(i, f, d, e, a, which):
+        dx, dy = (d, e) if f == 0 else (e, d)
+        s = ctx_of(a, (x + dx) % X, (y + dy) % Y, which) * 2 + f
         total = None
         for b in range(2):
             rel = row_block[s] - base[b] + 1
@@ -340,82 +333,111 @@
             total = part if total is None else total + part
         return total
 
-    def one_peer(i, d):
-        return x_peer(d) if i == 0 else y_peer(d)
-
-    order = [(d, i) for d in (2, 1, 3, 0) for i in range(2)]
+    def one_peer(f, d):
+        return x_peer(d) if f == 0 else y_peer(d)
+
+    order = [(d, f) for d in (2, 1, 3, 0) for f in range(2)]
     r0 = {}
-    for d, i in order:
-        def assemble(e, carry):
+
+    def assemble(i):
+        for d, f in order:
+            def fill(e, carry):
+                for a in range(ZH):
+                    out_core[i, f, d, e, a] = piece(i, f, d, e, a, 1 - core).astype(bf16)
+                return carry
+
+            lax.fori_loop(0, 4, fill, 0)
+            r0[i, f, d] = go(remote(
+                out_core.at[i, f, d], in_core.at[i, f, d],
+                r0_send.at[i, f, d], r0_recv.at[i, f, d], sibling,
+            ))
+
+    def r1(i, f, d, e):
+        return remote(
+            held.at[i, f, d, e], in_one.at[i, f, d - 1, e], r1_send.at[i, f, d - 1, e],
+            r1_recv.at[i, f, d - 1, e], one_peer(f, d),
+        )
+
+    def join(i):
+        for d, f in order:
+            r0[i, f, d].wait_recv()
+
+            def add(n, carry):
+                e = (n + 1) % 4
+                for a in range(ZH):
+                    total = piece(i, f, d, e, a, core) + in_core[i, f, d, e, a].astype(f32)
+                    held[i, f, d, e, a] = total.astype(bf16)
+                if d > 0:
+                    r1(i, f, d, e).start()
+                return carry
+
+            lax.fori_loop(0, 4, add, 0)
+
+    def back_part(b, part, first, dq_t):
+        keys = kwin[b, part, :]
+        dp = mm(vwin[b, part, :], gh[b], 1, 1)
+        ds = (w_scr[b, part, :].astype(f32) * (dp - delta[b])).astype(bf16)
+        dk = mm(ds, qs[b], 1, 0)
+        dk_rel[b, pl.ds(first + 1, dk.shape[0] // BLOCK)] = dk.reshape(-1, BLOCK, HEAD)
+        return dq_t + mm(keys, ds, 0, 0)
+
+    def back(b):
+        def step(tile, dq_t):
+            return back_part(b, keys_of(tile), tile * (TILE // BLOCK), dq_t)
+
+        dq_t = back_part(b, tail, BACK, jnp.zeros((HEAD, LANES), f32))
+        dq_t = lax.fori_loop(0, TILES, step, dq_t, unroll=TILES)
+        dq = (dq_t * (inverse[b] * SCALE)).T.astype(bf16)
+        for h in range(GROUP):
+            g_in[pl.ds(b * BLOCK, BLOCK), pl.ds(h * HEAD, HEAD)] = dq[h * BLOCK : (h + 1) * BLOCK]
+
+    assemble(1)
+    back(0)
+    join(1)
+    back(1)
+    assemble(0)
+    send_rows(1, g_in, dq_o)
+    join(0)
+
+    def r2(i, f, e):
+        return remote(
+            held_two.at[i, f, e], in_two.at[i, f, e - 1], r2_send.at[i, f, e - 1],
+            r2_recv.at[i, f, e - 1], one_peer(1 - f, e),
+        )
+
+    for i in (1, 0):
+        for e in (1, 2, 3, 0):
+            for f in range(2):
+                for d in (1, 3, 2):
+                    r1(i, f, d, e).wait_recv()
+                for a in range(ZH):
+                    total = held[i, f, 0, e, a].astype(f32)
+                    for d in range(3):
+                        total = total + in_one[i, f, d, e, a].astype(f32)
+                    held_two[i, f, e, a] = total.astype(bf16)
+                if e > 0:
+                    go(r2(i, f, e))
+
+    last = {}
+    for i in (1, 0):
+        for f in range(2):
+            for e in (1, 2, 3):
+                r2(i, f, e).wait_recv()
             for a in range(ZH):
-                for half in range(2):
-                    out_core[i, d, e, a, half] = piece(i, d, e, a, 1 - core, half).astype(bf16)
-            return carry
-
-        lax.fori_loop(0, 4, assemble, 0)
-        r0[i, d] = go(remote(
-            out_core.at[i, d], in_core.at[i, d], r0_send.at[i, d], r0_recv.at[i, d], sibling
-        ))
-    send_rows(1, g_in, dq_o)
-
-    def r1(i, d, e):
-        return remote(
-            held.at[i, d, e], in_one.at[i, d - 1, e], r1_send.at[i, d - 1, e],
-            r1_recv.at[i, d - 1, e], one_peer(i, d),
-        )
-
-    for d, i in order:
-        r0[i, d].wait_recv()
-
-        def add(n, carry):
-            e = (n + 1) % 4
-            for a in range(ZH):
-                for half in range(2):
-                    total = piece(i, d, e, a, core, half) + in_core[i, d, e, a, half].astype(f32)
-                    held[i, d, e, a, half] = total.astype(bf16)
-            if d > 0:
-                r1(i, d, e).start()
-            return carry
-
-        lax.fori_loop(0, 4, add, 0)
-
-    def r2(i, e):
-        return remote(
-            held_two.at[i, e], in_two.at[i, e - 1], r2_send.at[i, e - 1], r2_recv.at[i, e - 1],
-            one_peer(1 - i, e),
-        )
-
-    for e in (1, 2, 3, 0):
-        for i in range(2):
-            for d in (1, 3, 2):
-                r1(i, d, e).wait_recv()
-            for a in range(ZH):
-                total = held[i, 0, e, a].astype(f32)
-                for d in range(3):
-                    total = total + in_one[i, d, e, a].astype(f32)
-                held_two[i, e, a] = total.astype(bf16)
-            if e > 0:
-                go(r2(i, e))
-
-    last = []
-    for i in range(2):
-        for e in (1, 2, 3):
-            r2(i, e).wait_recv()
-        for a in range(ZH):
-            total = held_two[i, 0, a].astype(f32)
-            for e in range(3):
-                total = total + in_two[i, e, a].astype(f32)
-            held_z[i, a] = total.astype(bf16)
+                total = held_two[i, f, 0, a].astype(f32)
+                for e in range(3):
+                    total = total + in_two[i, f, e, a].astype(f32)
+                held_z[i, a, f] = total.astype(bf16)
         for n, peer in enumerate(peers):
             a = (zh + (n + 1) // TP) % ZH
-            last.append(go(remote(
+            last[i, n] = go(remote(
                 held_z.at[i, a, peer[1] // 2, pl.ds(pl.multiple_of((peer[1] % 2) * MINE, MINE), MINE), :],
                 in_fin.at[i, zh, t], r3_send.at[i, n], r3_recv.at[i, n], peer,
-            )))
+            ))
         in_fin[i, zh, t] = held_z[i, zh, t // 2, mine, :]
-    for i, out in enumerate((dk_o, dv_o)):
+    for i, out in ((1, dv_o), (0, dk_o)):
         for n in range(len(peers)):
-            last[i * len(peers) + n].wait_recv()
+            last[i, n].wait_recv()
         for h in range(TP):
             total = in_fin[i, 0, h].astype(f32) + in_fin[i, 1, h].astype(f32)
             out[:, pl.ds(h * HEAD, HEAD)] = total.astype(bf16)
@@ -426,9 +448,10 @@
     for copy in sends:
         copy.wait_send()
     for i in range(2):
-        for d in range(1, 4):
-            for e in range(4):
-                r1(i, d, e).wait_send()
+        for f in range(2):
+            for d in range(1, 4):
+                for e in range(4):
+                    r1(i, f, d, e).wait_send()
 
 
 def fused(doc_lengths, row_block, queries, keys, values, out_grad):
@@ -438,7 +461,7 @@
     smem = pl.BlockSpec(memory_space=pltpu.SMEM)
     V = pltpu.VMEM
     slots = (ZH, X, Y, CORE, 2, BLOCK, HEAD)
-    piece = (2, BLOCK, HEAD)
+    piece = (BLOCK, HEAD)
     number = jnp.arange(NBLK, dtype=jnp.int32)
     found = row_block[None, :] == number[:, None]
     slot_of = jnp.sum(jnp.where(found, number[None, :], 0), axis=1)
@@ -460,10 +483,10 @@
             V((2, LANES, HEAD), bf16), V((2, LANES, HEAD), bf16),
             V((2, WINDOW, LANES), f32), V((2, WINDOW, LANES), bf16),
             V((2, BACK + 3, BLOCK, HEAD), f32), V((2, BACK + 3, BLOCK, HEAD), f32),
-            V((2, 4, 4, ZH) + piece, bf16), V((2, 4, 4, ZH) + piece, bf16),
-            V((2, 4, 4, ZH) + piece, bf16), V((2, 3, 4, ZH) + piece, bf16),
-            V((2, 4, ZH) + piece, bf16), V((2, 3, ZH) + piece, bf16),
-            V((2, ZH) + piece, bf16), V((2, ZH, TP, MINE, HEAD), bf16),
+            V((2, 2, 4, 4, ZH) + piece, bf16), V((2, 2, 4, 4, ZH) + piece, bf16),
+            V((2, 2, 4, 4, ZH) + piece, bf16), V((2, 2, 3, 4, ZH) + piece, bf16),
+            V((2, 2, 4, ZH) + piece, bf16), V((2, 2, 3, ZH) + piece, bf16),
+            V((2, ZH, 2) + piece, bf16), V((2, ZH, TP, MINE, HEAD), bf16),
             dma((7,)),
             dma((7, 2)), dma((7, 2)),
             dma((2, 3)), dma((2, 3)),
@@ -471,9 +494,9 @@
             dma((2, 4, 3)), dma((2, 4, 3)),
             dma((2, 4, 4)), dma((2, 4, 4)),
             dma((2, 3)), dma((2, 3)),
-            dma((2, 4)), dma((2, 4)),
-            dma((2, 3, 4)), dma((2, 3, 4)),
-            dma((2, 3)), dma((2, 3)),
+            dma((2, 2, 4)), dma((2, 2, 4)),
+            dma((2, 2, 3, 4)), dma((2, 2, 3, 4)),
+            dma((2, 2, 3)), dma((2, 2, 3)),
             dma((2, 7)), dma((2, 7)),
         ],
         compiler_params=pltpu.CompilerParams(

time: 79.5 us -> 74 us (0.931)
  Pallas kernels: 77.4 us -> 72 us
    pallas_call x1, Pallas kernels: 75.6 us -> 70.2 us  [fused(): pl.pallas_call(fused_kernel, out_shape=(jax.ShapeDtypeStruct((MINE, TP *...]
where the time goes in v3:
time: 74 us; the launch traced here: 73.9 us
  Pallas kernels  72 us (97%)
  other arithmetic  1.28 us (2%)
    pallas_call x1, Pallas kernels, fused(): pl.pallas_call(fused_kernel, out_shape=(jax.ShapeDtypeStruct((MINE, TP *...  70.2 us
    pallas_call x1, Pallas kernels, hand_over(): pl.pallas_call(hand_over_kernel, out_shape=tuple((jax.ShapeDtypeStruct(a....  1.82 us

profile of v3, /device:TPU:1, one launch (start us, length us, event | category | flops | bytes accessed | tf_op | source)
XLA Modules:
  0.0 73.9 jit_solution(4491232306124235030)
XLA Ops:
  0.6 1.3 %select_reduce_fusion.slot_of = s32[128]{0:T(128)} fusion(s32[128]{0:T(128)} %row_block.1), kind=kLoop, calls=%fused_computation | loop fusion | flops 49024 | bytes 1024 | tf_op jit(solution)/shard_map/reduce_sum | solution.py:467
  1.9 70.2 %fused.1 = (bf16[32,4096]{1,0:T(8,128)(2,1)}, bf16[32,4096]{1,0:T(8,128)(2,1)}, bf16[32,512]{1,0:T(8,128)(2,1)}, bf16[32,512]{1,0:T(8,128)(2,1)}) custom-call(s32[16]{0:T(128)} %doc.1, s32[128]{0:T(128)} %row_block.1, s32[128]{0:T(128)} %select_reduce_fusion.slot_of, bf16[32,4096]{1,0:T(8,128)(2,1)} %q.1, bf16[32,512]{1,0:T(8,128)(2,1)} %k.1, ...), custom_call_target="tpu_custom_call" | custom-call | tf_op jit(solution)/shard_map/fused/pallas_call | solution.py:468
  72.1 1.8 %hand_over.1 = (bf16[32,4096]{1,0:T(8,128)(2,1)}, bf16[32,4096]{1,0:T(8,128)(2,1)}, bf16[32,512]{1,0:T(8,128)(2,1)}, bf16[32,512]{1,0:T(8,128)(2,1)}) custom-call(bf16[32,4096]{1,0:T(8,128)(2,1)} %get-tuple-element.8.refs_0_, bf16[32,4096]{1,0:T(8,128)(2,1)} %get-tuple-element.9.refs_1_, bf16[32,512]{1,0:T(8,128)(2,1)} %get-tuple-element.10.refs_2_, ...), custom_call_target="tpu_custom_call" | custom-call | tf_op jit(solution)/shard_map/hand_over/pallas_call | solution.py:524

commit v4 on v3

--- a/solution.py
+++ b/solution.py
@@ -83,9 +83,9 @@
 
 
 def fused_kernel(
-    doc, row_block, slot_of, q, k, v, g, att_o, dq_o, dk_o, dv_o,
+    doc, row_block, slot_of, q, k, v, g, att_o, dq_o, fin_k, fin_v,
     kbuf, vbuf, q_in, g_in, kwin, vwin, qh, gh, qs, gs, s_scr, w_scr, dk_rel, dv_rel,
-    out_core, in_core, held, in_one, held_two, in_two, held_z, in_fin,
+    out_core, in_core, held, in_one, held_two, in_two, held_z,
     own_sem, tp_send, tp_recv, wide_send, wide_recv, one_send, one_recv, two_send, two_recv,
     core_send, core_recv, res_send, res_recv, r0_send, r0_recv, r1_send, r1_recv,
     r2_send, r2_recv, r3_send, r3_recv,
@@ -108,96 +108,93 @@
     def y_peer(d):
         return (ctx_of(zh, x, (y + d) % Y, core), t)
 
-    bufs = (kbuf, vbuf)
+    bufs, fins = (kbuf, vbuf), (fin_k, fin_v)
 
     mine = pl.ds(pl.multiple_of((t % 2) * MINE, MINE), MINE)
-    small = []
-    for n, peer in enumerate(peers):
-        for i, ref in enumerate((k, v)):
-            small.append(go(remote(
-                ref.at[:, columns(peer[1], HEAD)],
-                bufs[i].at[zh, x, y, core, t // 2, mine, :],
-                tp_send.at[n, i], tp_recv.at[n, i], peer,
-            )))
-    local = []
+    small = {}
+    local = {}
     for i, ref in enumerate((k, v)):
-        local.append(pltpu.make_async_copy(
-            ref.at[:, columns(t, HEAD)], bufs[i].at[zh, x, y, core, t // 2, mine, :], own_sem.at[i]
+        to = bufs[i].at[zh, x, y, core, t // 2, mine, :]
+        for n, peer in enumerate(peers):
+            small[i, n] = go(remote(
+                ref.at[:, columns(peer[1], HEAD)], to, tp_send.at[i, n], tp_recv.at[i, n], peer
+            ))
+        local[i] = pltpu.make_async_copy(ref.at[:, columns(t, HEAD)], to, own_sem.at[i])
+        local[i].start()
+    for i, (ref, to) in enumerate(((q, q_in), (g, g_in))):
+        local[2 + i] = pltpu.make_async_copy(
+            ref.at[:, columns(t, WIDE)], to.at[rows_of(t, MINE), :], own_sem.at[2 + i]
+        )
+        local[2 + i].start()
+
+    def one_peer(f, d):
+        return x_peer(d) if f == 0 else y_peer(d)
+
+    firsts, seconds, siblings, wide = {}, {}, {}, {}
+
+    def spread(i, f, d):
+        dx, dy = (-d, 0) if f == 0 else (0, -d)
+        here = bufs[i].at[:, (x + dx) % X, (y + dy) % Y, core, f]
+        for e in (2, 1, 3):
+            seconds[i, f, d, e] = go(remote(
+                here, here, two_send.at[i, f, d, e - 1], two_recv.at[i, f, d, e - 1],
+                one_peer(1 - f, e),
+            ))
+
+    def to_sibling(i, f, e):
+        for d in range(4):
+            if e > 0:
+                seconds[i, f, d, e].wait_recv()
+        if f == 0:
+            here = bufs[i].at[:, :, (y - e) % Y, core, f]
+        else:
+            here = bufs[i].at[:, (x - e) % X, :, core, f]
+        siblings[i, f, e] = go(remote(
+            here, here, core_send.at[i, f, e], core_recv.at[i, f, e], sibling
         ))
-    for i, (ref, to) in enumerate(((q, q_in), (g, g_in))):
-        local.append(pltpu.make_async_copy(
-            ref.at[:, columns(t, WIDE)], to.at[rows_of(t, MINE), :], own_sem.at[2 + i]
-        ))
-    for copy in local:
-        copy.start()
-
-    for copy in small:
-        copy.wait_recv()
-    local[0].wait()
-    local[1].wait()
-
-    def chunk(i, dx, dy):
-        return bufs[i].at[:, (x + dx) % X, (y + dy) % Y, core]
-
-    firsts = {}
-    for d in (2, 1, 3):
-        for i in range(2):
-            here = chunk(i, 0, 0)
-            firsts[i, d] = go(remote(
-                here, here, one_send.at[i, d - 1], one_recv.at[i, d - 1],
-                x_peer(d) if i == 0 else y_peer(d),
-            ))
-
-    wide = []
+
+    for i in range(2):
+        for n in range(len(peers)):
+            small[i, n].wait_recv()
+        local[i].wait()
+        for d in (2, 1, 3):
+            for f in range(2):
+                here = bufs[i].at[:, x, y, core, f]
+                firsts[i, f, d] = go(remote(
+                    here, here, one_send.at[i, f, d - 1], one_recv.at[i, f, d - 1], one_peer(f, d)
+                ))
+        for f in range(2):
+            spread(i, f, 0)
     for i, (ref, to) in enumerate(((q, q_in), (g, g_in))):
         for d in (2, 1, 3):
             peer = (t + d) % TP
-            wide.append(go(remote(
+            wide[i, d] = go(remote(
                 ref.at[:, columns(peer, WIDE)], to.at[rows_of(t, MINE), :],
                 wide_send.at[i, d - 1], wide_recv.at[i, d - 1], (c, peer),
-            )))
-
-    seconds = {}
-    siblings = []
-
-    def to_sibling(i, d, e):
-        dx, dy = (-d, -e) if i == 0 else (-e, -d)
-        here = chunk(i, dx, dy)
-        siblings.append(go(remote(
-            here, here, core_send.at[i, d, e], core_recv.at[i, d, e], sibling
-        )))
-
-    def spread(i, d):
-        dx, dy = (-d, 0) if i == 0 else (0, -d)
-        here = chunk(i, dx, dy)
-        for e in (2, 1, 3):
-            seconds[i, d, e] = go(remote(
-                here, here, two_send.at[i, d, e - 1], two_recv.at[i, d, e - 1],
-                y_peer(e) if i == 0 else x_peer(e),
             ))
-        to_sibling(i, d, 0)
-
-    spread(0, 0)
-    spread(1, 0)
-    for d in (1, 3, 2):
-        for i in range(2):
-            firsts[i, d].wait_recv()
-            spread(i, d)
-    for d in (0, 1, 3, 2):
-        for e in (1, 3, 2):
-            for i in range(2):
-                seconds[i, d, e].wait_recv()
-                to_sibling(i, d, e)
-
-    for copy in wide:
-        copy.wait_recv()
-    local[2].wait()
-    local[3].wait()
-    for b in range(2):
-        here = pl.ds(b * BLOCK, BLOCK)
-        for h in range(GROUP):
-            qh[b, pl.ds(h * BLOCK, BLOCK), :] = q_in[here, pl.ds(h * HEAD, HEAD)]
-            gh[b, pl.ds(h * BLOCK, BLOCK), :] = g_in[here, pl.ds(h * HEAD, HEAD)]
+    for i in range(2):
+        for d in (1, 3, 2):
+            for f in range(2):
+                firsts[i, f, d].wait_recv()
+                spread(i, f, d)
+    for f in range(2):
+        to_sibling(0, f, 0)
+    for e in (1, 3, 2):
+        for f in range(2):
+            to_sibling(0, f, e)
+    for f in range(2):
+        to_sibling(1, f, 0)
+
+    def by_head(i, ref, to):
+        for d in (1, 2, 3):
+            wide[i, d].wait_recv()
+        local[2 + i].wait()
+        for b in range(2):
+            here = pl.ds(b * BLOCK, BLOCK)
+            for h in range(GROUP):
+                to[b, pl.ds(h * BLOCK, BLOCK), :] = ref[here, pl.ds(h * HEAD, HEAD)]
+
+    by_head(0, q_in, qh)
 
     offset = lax.broadcasted_iota(jnp.int32, (1, LANES), 1) % BLOCK
     base, low = [], []
@@ -212,19 +209,24 @@
         base.append(block - BACK)
         low.append(lowest - (block - BACK) * BLOCK)
 
-    for copy in siblings:
-        copy.wait_recv()
-
-    def window(j, carry):
-        to = pl.ds(pl.multiple_of(j * BLOCK, BLOCK), BLOCK)
-        for b in range(2):
-            s = slot_of[jnp.maximum(base[b] + j, 0)]
-            at = tuple(lax.rem(lax.div(s, n), m) for n, m in ((64, 2), (16, 4), (4, 4), (2, 2), (1, 2)))
-            kwin[b, to, :] = kbuf[at]
-            vwin[b, to, :] = vbuf[at]
-        return carry
-
-    lax.fori_loop(0, BACK + 1, window, 0)
+    def in_order(i, to):
+        for f in range(2):
+            for e in range(4):
+                siblings[i, f, e].wait_recv()
+
+        def window(j, carry):
+            rows = pl.ds(pl.multiple_of(j * BLOCK, BLOCK), BLOCK)
+            for b in range(2):
+                s = slot_of[jnp.maximum(base[b] + j, 0)]
+                at = tuple(
+                    lax.rem(lax.div(s, n), m) for n, m in ((64, 2), (16, 4), (4, 4), (2, 2), (1, 2))
+                )
+                to[b, rows, :] = bufs[i][at]
+            return carry
+
+        lax.fori_loop(0, BACK + 1, window, 0)
+
+    in_order(0, kwin)
 
     def keys_of(tile):
         return pl.ds(pl.multiple_of(tile * TILE, TILE), TILE)
@@ -254,6 +256,12 @@
         tops.append(folded(s, jnp.max))
     tops = lax.fori_loop(0, TILES, scores, tuple(tops), unroll=TILES)
     tops = [jnp.max(top, axis=0, keepdims=True) for top in tops]
+
+    for e in (1, 3, 2):
+        for f in range(2):
+            to_sibling(1, f, e)
+    by_head(1, g_in, gh)
+    in_order(1, vwin)
 
     def weigh_part(b, part, total, acc):
         w = jnp.exp2((s_scr[b, part, :] - tops[b]) * SCALE2)
@@ -296,11 +304,10 @@
                 ref.at[rows_of(peer, MINE), :], out.at[:, columns(t, WIDE)],
                 res_send.at[i, d - 1], res_recv.at[i, d - 1], (c, peer),
             )))
-        copy = pltpu.make_async_copy(
-            ref.at[rows_of(t, MINE), :], out.at[:, columns(t, WIDE)], own_sem.at[5 + i]
+        local[4 + i] = pltpu.make_async_copy(
+            ref.at[rows_of(t, MINE), :], out.at[:, columns(t, WIDE)], own_sem.at[4 + i]
         )
-        copy.start()
-        local.append(copy)
+        local[4 + i].start()
 
     send_rows(0, q_in, att_o)
 
@@ -333,9 +340,6 @@
             total = part if total is None else total + part
         return total
 
-    def one_peer(f, d):
-        return x_peer(d) if f == 0 else y_peer(d)
-
     order = [(d, f) for d in (2, 1, 3, 0) for f in range(2)]
     r0 = {}
 
@@ -392,8 +396,8 @@
             g_in[pl.ds(b * BLOCK, BLOCK), pl.ds(h * HEAD, HEAD)] = dq[h * BLOCK : (h + 1) * BLOCK]
 
     assemble(1)
+    join(1)
     back(0)
-    join(1)
     back(1)
     assemble(0)
     send_rows(1, g_in, dq_o)
@@ -432,19 +436,18 @@
             a = (zh + (n + 1) // TP) % ZH
             last[i, n] = go(remote(
                 held_z.at[i, a, peer[1] // 2, pl.ds(pl.multiple_of((peer[1] % 2) * MINE, MINE), MINE), :],
-                in_fin.at[i, zh, t], r3_send.at[i, n], r3_recv.at[i, n], peer,
+                fins[i].at[zh, t], r3_send.at[i, n], r3_recv.at[i, n], peer,
             ))
-        in_fin[i, zh, t] = held_z[i, zh, t // 2, mine, :]
-    for i, out in ((1, dv_o), (0, dk_o)):
-        for n in range(len(peers)):
-            last[i, n].wait_recv()
-        for h in range(TP):
-            total = in_fin[i, 0, h].astype(f32) + in_fin[i, 1, h].astype(f32)
-            out[:, pl.ds(h * HEAD, HEAD)] = total.astype(bf16)
+        local[6 + i] = pltpu.make_async_copy(
+            held_z.at[i, zh, t // 2, mine, :], fins[i].at[zh, t], own_sem.at[6 + i]
+        )
+        local[6 + i].start()
+    for copy in last.values():
+        copy.wait_recv()
     for copy in results:
         copy.wait_recv()
-    for copy in local[4:]:
-        copy.wait()
+    for i in range(4, 8):
+        local[i].wait()
     for copy in sends:
         copy.wait_send()
     for i in range(2):
@@ -457,7 +460,6 @@
 def fused(doc_lengths, row_block, queries, keys, values, out_grad):
     dma = pltpu.SemaphoreType.DMA
     anywhere = pl.BlockSpec(memory_space=pl.ANY)
-    vmem = pl.BlockSpec(memory_space=pltpu.VMEM)
     smem = pl.BlockSpec(memory_space=pltpu.SMEM)
     V = pltpu.VMEM
     slots = (ZH, X, Y, CORE, 2, BLOCK, HEAD)
@@ -470,11 +472,11 @@
         out_shape=(
             jax.ShapeDtypeStruct((MINE, TP * WIDE), bf16),
             jax.ShapeDtypeStruct((MINE, TP * WIDE), bf16),
-            jax.ShapeDtypeStruct((MINE, TP * HEAD), bf16),
-            jax.ShapeDtypeStruct((MINE, TP * HEAD), bf16),
+            jax.ShapeDtypeStruct((ZH, TP, MINE, HEAD), bf16),
+            jax.ShapeDtypeStruct((ZH, TP, MINE, HEAD), bf16),
         ),
         in_specs=[smem, smem, smem] + [anywhere] * 4,
-        out_specs=[anywhere] * 2 + [vmem] * 2,
+        out_specs=[anywhere] * 4,
         scratch_shapes=[
             V(slots, bf16), V(slots, bf16),
             V((ROWS, WIDE), bf16), V((ROWS, WIDE), bf16),
@@ -486,13 +488,13 @@
             V((2, 2, 4, 4, ZH) + piece, bf16), V((2, 2, 4, 4, ZH) + piece, bf16),
             V((2, 2, 4, 4, ZH) + piece, bf16), V((2, 2, 3, 4, ZH) + piece, bf16),
             V((2, 2, 4, ZH) + piece, bf16), V((2, 2, 3, ZH) + piece, bf16),
-            V((2, ZH, 2) + piece, bf16), V((2, ZH, TP, MINE, HEAD), bf16),
-            dma((7,)),
-            dma((7, 2)), dma((7, 2)),
+            V((2, ZH, 2) + piece, bf16),
+            dma((8,)),
+            dma((2, 7)), dma((2, 7)),
             dma((2, 3)), dma((2, 3)),
-            dma((2, 3)), dma((2, 3)),
-            dma((2, 4, 3)), dma((2, 4, 3)),
-            dma((2, 4, 4)), dma((2, 4, 4)),
+            dma((2, 2, 3)), dma((2, 2, 3)),
+            dma((2, 2, 4, 3)), dma((2, 2, 4, 3)),
+            dma((2, 2, 4)), dma((2, 2, 4)),
             dma((2, 3)), dma((2, 3)),
             dma((2, 2, 4)), dma((2, 2, 4)),
             dma((2, 2, 3, 4)), dma((2, 2, 3, 4)),
@@ -507,13 +509,18 @@
 
 
 def hand_over_kernel(*refs):
-    held, sems = refs[8:12], refs[12]
+    held, sums, sems = refs[8:12], refs[12:14], refs[14]
     arrive = [pltpu.make_async_copy(refs[i], held[i], sems.at[0, i]) for i in range(4)]
-    leave = [pltpu.make_async_copy(held[i], refs[4 + i], sems.at[1, i]) for i in range(4)]
+    from_where = held[:2] + sums
+    leave = [pltpu.make_async_copy(from_where[i], refs[4 + i], sems.at[1, i]) for i in range(4)]
     for copy in arrive:
         copy.start()
     for i in range(4):
         arrive[i].wait()
+        if i >= 2:
+            for h in range(TP):
+                total = held[i][0, h].astype(f32) + held[i][1, h].astype(f32)
+                sums[i - 2][:, pl.ds(h * HEAD, HEAD)] = total.astype(bf16)
         leave[i].start()
     for copy in leave:
         copy.wait()
@@ -521,12 +528,14 @@
 
 def hand_over(arrays):
     anywhere = pl.BlockSpec(memory_space=pl.ANY)
+    narrow = jax.ShapeDtypeStruct((MINE, TP * HEAD), bf16)
     return pl.pallas_call(
         hand_over_kernel,
-        out_shape=tuple(jax.ShapeDtypeStruct(a.shape, a.dtype) for a in arrays),
+        out_shape=tuple(jax.ShapeDtypeStruct(a.shape, a.dtype) for a in arrays[:2]) + (narrow,) * 2,
         in_specs=[anywhere] * 4,
         out_specs=[anywhere] * 4,
         scratch_shapes=[pltpu.VMEM(a.shape, a.dtype) for a in arrays]
+        + [pltpu.VMEM(narrow.shape, bf16)] * 2
         + [pltpu.SemaphoreType.DMA((2, 4))],
         name="hand_over",
     )(*arrays)

time: 74 us -> 71.6 us (0.968)
  Pallas kernels: 72 us -> 69.5 us
    pallas_call x1, Pallas kernels: 70.2 us -> 67.7 us  [fused(): pl.pallas_call(fused_kernel, out_shape=(jax.ShapeDtypeStruct((MINE, TP *...]
where the time goes in v4:
time: 71.6 us; the launch traced here: 71.5 us
  Pallas kernels  69.5 us (97%)
  other arithmetic  1.28 us (2%)
    pallas_call x1, Pallas kernels, fused(): pl.pallas_call(fused_kernel, out_shape=(jax.ShapeDtypeStruct((MINE, TP *...  67.7 us
    pallas_call x1, Pallas kernels, hand_over(): pl.pallas_call(hand_over_kernel, out_shape=tuple((jax.ShapeDtypeStruct(a....  1.82 us

profile of v4, /device:TPU:1, one launch (start us, length us, event | category | flops | bytes accessed | tf_op | source)
XLA Modules:
  0.0 71.5 jit_solution(9586123519131296545)
XLA Ops:
  0.6 1.3 %select_reduce_fusion.slot_of = s32[128]{0:T(128)} fusion(s32[128]{0:T(128)} %row_block.1), kind=kLoop, calls=%fused_computation | loop fusion | flops 49024 | bytes 1024 | tf_op jit(solution)/shard_map/reduce_sum | solution.py:469
  1.9 67.7 %fused.1 = (bf16[32,4096]{1,0:T(8,128)(2,1)}, bf16[32,4096]{1,0:T(8,128)(2,1)}, bf16[2,4,32,128]{3,2,1,0:T(8,128)(2,1)}, bf16[2,4,32,128]{3,2,1,0:T(8,128)(2,1)}) custom-call(s32[16]{0:T(128)} %doc.1, s32[128]{0:T(128)} %row_block.1, s32[128]{0:T(128)} %select_reduce_fusion.slot_of, bf16[32,4096]{1,0:T(8,128)(2,1)} %q.1, bf16[32,512]{1,0:T(8,128)(2,1)} %k.1, ...), custom_call_target="tpu_custom_call" | custom-call | tf_op jit(solution)/shard_map/fused/pallas_call | solution.py:470
  69.6 1.8 %hand_over.1 = (bf16[32,4096]{1,0:T(8,128)(2,1)}, bf16[32,4096]{1,0:T(8,128)(2,1)}, bf16[32,512]{1,0:T(8,128)(2,1)}, bf16[32,512]{1,0:T(8,128)(2,1)}) custom-call(bf16[32,4096]{1,0:T(8,128)(2,1)} %get-tuple-element.8.refs_0_, bf16[32,4096]{1,0:T(8,128)(2,1)} %get-tuple-element.9.refs_1_, bf16[2,4,32,128]{3,2,1,0:T(8,128)(2,1)} %get-tuple-element.10.refs_2_, ...), custom_call_target="tpu_custom_call" | custom-call | tf_op jit(solution)/shard_map/hand_over/pallas_call | solution.py:532

commit v5 on v4

--- a/solution.py
+++ b/solution.py
@@ -135,16 +135,26 @@
     def spread(i, f, d):
         dx, dy = (-d, 0) if f == 0 else (0, -d)
         here = bufs[i].at[:, (x + dx) % X, (y + dy) % Y, core, f]
-        for e in (2, 1, 3):
+        for e in (1, 3):
             seconds[i, f, d, e] = go(remote(
-                here, here, two_send.at[i, f, d, e - 1], two_recv.at[i, f, d, e - 1],
+                here, here, two_send.at[i, f, d, e], two_recv.at[i, f, d, e], one_peer(1 - f, e)
+            ))
+
+    def relay(i, f, d):
+        for a, e in ((0, 1), (1, 3)):
+            seconds[i, f, d, e].wait_recv()
+            dx, dy = (-d, -e) if f == 0 else (-e, -d)
+            here = bufs[i].at[a, (x + dx) % X, (y + dy) % Y, core, f]
+            seconds[i, f, d, 2 * a] = go(remote(
+                here, here, two_send.at[i, f, d, 2 * a], two_recv.at[i, f, d, 2 * a],
                 one_peer(1 - f, e),
             ))
 
     def to_sibling(i, f, e):
         for d in range(4):
-            if e > 0:
-                seconds[i, f, d, e].wait_recv()
+            if e == 2:
+                seconds[i, f, d, 0].wait_recv()
+                seconds[i, f, d, 2].wait_recv()
         if f == 0:
             here = bufs[i].at[:, :, (y - e) % Y, core, f]
         else:
@@ -153,7 +163,7 @@
             here, here, core_send.at[i, f, e], core_recv.at[i, f, e], sibling
         ))
 
-    for i in range(2):
+    def begin(i):
         for n in range(len(peers)):
             small[i, n].wait_recv()
         local[i].wait()
@@ -165,6 +175,13 @@
                 ))
         for f in range(2):
             spread(i, f, 0)
+
+    def go_on(i, d):
+        for f in range(2):
+            firsts[i, f, d].wait_recv()
+            spread(i, f, d)
+
+    begin(0)
     for i, (ref, to) in enumerate(((q, q_in), (g, g_in))):
         for d in (2, 1, 3):
             peer = (t + d) % TP
@@ -172,18 +189,19 @@
                 ref.at[:, columns(peer, WIDE)], to.at[rows_of(t, MINE), :],
                 wide_send.at[i, d - 1], wide_recv.at[i, d - 1], (c, peer),
             ))
+    begin(1)
     for i in range(2):
         for d in (1, 3, 2):
+            go_on(i, d)
+    for i in range(2):
+        for d in (0, 1, 3, 2):
             for f in range(2):
-                firsts[i, f, d].wait_recv()
-                spread(i, f, d)
+                relay(i, f, d)
+        for e in (0, 1, 3):
+            for f in range(2):
+                to_sibling(i, f, e)
     for f in range(2):
-        to_sibling(0, f, 0)
-    for e in (1, 3, 2):
-        for f in range(2):
-            to_sibling(0, f, e)
-    for f in range(2):
-        to_sibling(1, f, 0)
+        to_sibling(0, f, 2)
 
     def by_head(i, ref, to):
         for d in (1, 2, 3):
@@ -224,7 +242,7 @@
                 to[b, rows, :] = bufs[i][at]
             return carry
 
-        lax.fori_loop(0, BACK + 1, window, 0)
+        lax.fori_loop(0, BACK + 1, window, 0, unroll=11)
 
     in_order(0, kwin)
 
@@ -257,9 +275,8 @@
     tops = lax.fori_loop(0, TILES, scores, tuple(tops), unroll=TILES)
     tops = [jnp.max(top, axis=0, keepdims=True) for top in tops]
 
-    for e in (1, 3, 2):
-        for f in range(2):
-            to_sibling(1, f, e)
+    for f in range(2):
+        to_sibling(1, f, 2)
     by_head(1, g_in, gh)
     in_order(1, vwin)
 
@@ -280,22 +297,14 @@
     )
     state = lax.fori_loop(0, TILES, weigh, state, unroll=TILES)
 
-    inverse, delta = [], []
+    inverse, inv_rows, delta = [], [], []
+    for b in range(2):
+        inv = 1.0 / jnp.sum(state[b][0], axis=0, keepdims=True)
+        inverse.append(inv)
+        inv_rows.append(jnp.broadcast_to(inv, (HEAD, LANES)).T)
+        gs[b] = (gh[b].astype(f32) * inv_rows[b]).astype(bf16)
+
     results = []
-
-    for b in range(2):
-        total, acc = state[b]
-        inv = 1.0 / jnp.sum(total, axis=0, keepdims=True)
-        att_t = acc * inv
-        g_t = gh[b].astype(f32).T
-        delta.append(jnp.sum(g_t * att_t, axis=0, keepdims=True))
-        inverse.append(inv)
-        att = att_t.T.astype(bf16)
-        inv_rows = jnp.broadcast_to(inv, (HEAD, LANES)).T
-        gs[b] = (gh[b].astype(f32) * inv_rows).astype(bf16)
-        qs[b] = (qh[b].astype(f32) * (inv_rows * SCALE)).astype(bf16)
-        for h in range(GROUP):
-            q_in[pl.ds(b * BLOCK, BLOCK), pl.ds(h * HEAD, HEAD)] = att[h * BLOCK : (h + 1) * BLOCK]
 
     def send_rows(i, ref, out):
         for d in (2, 1, 3):
@@ -309,8 +318,6 @@
         )
         local[4 + i].start()
 
-    send_rows(0, q_in, att_o)
-
     def value_part(b, part, first):
         dv = mm(w_scr[b, part, :], gs[b], 1, 0)
         dv_rel[b, pl.ds(first + 1, dv.shape[0] // BLOCK)] = dv.reshape(-1, BLOCK, HEAD)
@@ -350,7 +357,7 @@
                     out_core[i, f, d, e, a] = piece(i, f, d, e, a, 1 - core).astype(bf16)
                 return carry
 
-            lax.fori_loop(0, 4, fill, 0)
+            lax.fori_loop(0, 4, fill, 0, unroll=4)
             r0[i, f, d] = go(remote(
                 out_core.at[i, f, d], in_core.at[i, f, d],
                 r0_send.at[i, f, d], r0_recv.at[i, f, d], sibling,
@@ -375,7 +382,7 @@
                     r1(i, f, d, e).start()
                 return carry
 
-            lax.fori_loop(0, 4, add, 0)
+            lax.fori_loop(0, 4, add, 0, unroll=4)
 
     def back_part(b, part, first, dq_t):
         keys = kwin[b, part, :]
@@ -396,6 +403,14 @@
             g_in[pl.ds(b * BLOCK, BLOCK), pl.ds(h * HEAD, HEAD)] = dq[h * BLOCK : (h + 1) * BLOCK]
 
     assemble(1)
+    for b in range(2):
+        att_t = state[b][1] * inverse[b]
+        delta.append(jnp.sum(gh[b].astype(f32).T * att_t, axis=0, keepdims=True))
+        att = att_t.T.astype(bf16)
+        qs[b] = (qh[b].astype(f32) * (inv_rows[b] * SCALE)).astype(bf16)
+        for h in range(GROUP):
+            q_in[pl.ds(b * BLOCK, BLOCK), pl.ds(h * HEAD, HEAD)] = att[h * BLOCK : (h + 1) * BLOCK]
+    send_rows(0, q_in, att_o)
     join(1)
     back(0)
     back(1)
@@ -493,7 +508,7 @@
             dma((2, 7)), dma((2, 7)),
             dma((2, 3)), dma((2, 3)),
             dma((2, 2, 3)), dma((2, 2, 3)),
-            dma((2, 2, 4, 3)), dma((2, 2, 4, 3)),
+            dma((2, 2, 4, 4)), dma((2, 2, 4, 4)),
             dma((2, 2, 4)), dma((2, 2, 4)),
             dma((2, 3)), dma((2, 3)),
             dma((2, 2, 4)), dma((2, 2, 4)),

time: 71.6 us -> 68.6 us (0.958)
  Pallas kernels: 69.5 us -> 66.3 us
    pallas_call x1, Pallas kernels: 67.7 us -> 64.5 us  [fused(): pl.pallas_call(fused_kernel, out_shape=(jax.ShapeDtypeStruct((MINE, TP *...]
where the time goes in v5:
time: 68.6 us; the launch traced here: 68.4 us
  Pallas kernels  66.3 us (97%)
  other arithmetic  1.28 us (2%)
  between operations  0.8 us (1%)
    pallas_call x1, Pallas kernels, fused(): pl.pallas_call(fused_kernel, out_shape=(jax.ShapeDtypeStruct((MINE, TP *...  64.5 us
    pallas_call x1, Pallas kernels, hand_over(): pl.pallas_call(hand_over_kernel, out_shape=tuple((jax.ShapeDtypeStruct(a....  1.82 us

profile of v5, /device:TPU:1, one launch (start us, length us, event | category | flops | bytes accessed | tf_op | source)
XLA Modules:
  0.0 68.4 jit_solution(8811888313970725823)
XLA Ops:
  0.6 1.3 %select_reduce_fusion.slot_of = s32[128]{0:T(128)} fusion(s32[128]{0:T(128)} %row_block.1), kind=kLoop, calls=%fused_computation | loop fusion | flops 49024 | bytes 1024 | tf_op jit(solution)/shard_map/reduce_sum | solution.py:484
  1.9 64.5 %fused.1 = (bf16[32,4096]{1,0:T(8,128)(2,1)}, bf16[32,4096]{1,0:T(8,128)(2,1)}, bf16[2,4,32,128]{3,2,1,0:T(8,128)(2,1)}, bf16[2,4,32,128]{3,2,1,0:T(8,128)(2,1)}) custom-call(s32[16]{0:T(128)} %doc.1, s32[128]{0:T(128)} %row_block.1, s32[128]{0:T(128)} %select_reduce_fusion.slot_of, bf16[32,4096]{1,0:T(8,128)(2,1)} %q.1, bf16[32,512]{1,0:T(8,128)(2,1)} %k.1, ...), custom_call_target="tpu_custom_call" | custom-call | tf_op jit(solution)/shard_map/fused/pallas_call | solution.py:485
  66.4 1.8 %hand_over.1 = (bf16[32,4096]{1,0:T(8,128)(2,1)}, bf16[32,4096]{1,0:T(8,128)(2,1)}, bf16[32,512]{1,0:T(8,128)(2,1)}, bf16[32,512]{1,0:T(8,128)(2,1)}) custom-call(bf16[32,4096]{1,0:T(8,128)(2,1)} %get-tuple-element.8.refs_0_, bf16[32,4096]{1,0:T(8,128)(2,1)} %get-tuple-element.9.refs_1_, bf16[2,4,32,128]{3,2,1,0:T(8,128)(2,1)} %get-tuple-element.10.refs_2_, ...), custom_call_target="tpu_custom_call" | custom-call | tf_op jit(solution)/shard_map/hand_over/pallas_call | solution.py:547

commit v6 on v5

--- a/solution.py
+++ b/solution.py
@@ -83,9 +83,9 @@
 
 
 def fused_kernel(
-    doc, row_block, slot_of, q, k, v, g, att_o, dq_o, fin_k, fin_v,
+    doc, row_block, row_vector, q, k, v, g, att_o, dq_o, fin_k, fin_v,
     kbuf, vbuf, q_in, g_in, kwin, vwin, qh, gh, qs, gs, s_scr, w_scr, dk_rel, dv_rel,
-    out_core, in_core, held, in_one, held_two, in_two, held_z,
+    slot_v, slot_of, out_core, in_core, held, in_one, held_two, in_two, held_z,
     own_sem, tp_send, tp_recv, wide_send, wide_recv, one_send, one_recv, two_send, two_recv,
     core_send, core_recv, res_send, res_recv, r0_send, r0_recv, r1_send, r1_recv,
     r2_send, r2_recv, r3_send, r3_recv,
@@ -126,6 +126,13 @@
             ref.at[:, columns(t, WIDE)], to.at[rows_of(t, MINE), :], own_sem.at[2 + i]
         )
         local[2 + i].start()
+
+    held_blocks = jnp.broadcast_to(row_vector[...], (NBLK, NBLK)).T
+    wanted = lax.broadcasted_iota(jnp.int32, (NBLK, NBLK), 1)
+    number = lax.broadcasted_iota(jnp.int32, (NBLK, NBLK), 0)
+    slot_v[...] = jnp.sum(jnp.where(held_blocks == wanted, number, 0), axis=0, keepdims=True)
+    to_scalars = pltpu.make_async_copy(slot_v, slot_of, own_sem.at[8])
+    to_scalars.start()
 
     def one_peer(f, d):
         return x_peer(d) if f == 0 else y_peer(d)
@@ -235,7 +242,7 @@
         def window(j, carry):
             rows = pl.ds(pl.multiple_of(j * BLOCK, BLOCK), BLOCK)
             for b in range(2):
-                s = slot_of[jnp.maximum(base[b] + j, 0)]
+                s = slot_of[0, jnp.maximum(base[b] + j, 0)]
                 at = tuple(
                     lax.rem(lax.div(s, n), m) for n, m in ((64, 2), (16, 4), (4, 4), (2, 2), (1, 2))
                 )
@@ -244,6 +251,7 @@
 
         lax.fori_loop(0, BACK + 1, window, 0, unroll=11)
 
+    to_scalars.wait()
     in_order(0, kwin)
 
     def keys_of(tile):
@@ -479,9 +487,6 @@
     V = pltpu.VMEM
     slots = (ZH, X, Y, CORE, 2, BLOCK, HEAD)
     piece = (BLOCK, HEAD)
-    number = jnp.arange(NBLK, dtype=jnp.int32)
-    found = row_block[None, :] == number[:, None]
-    slot_of = jnp.sum(jnp.where(found, number[None, :], 0), axis=1)
     return pl.pallas_call(
         fused_kernel,
         out_shape=(
@@ -490,7 +495,7 @@
             jax.ShapeDtypeStruct((ZH, TP, MINE, HEAD), bf16),
             jax.ShapeDtypeStruct((ZH, TP, MINE, HEAD), bf16),
         ),
-        in_specs=[smem, smem, smem] + [anywhere] * 4,
+        in_specs=[smem, smem, pl.BlockSpec(memory_space=pltpu.VMEM)] + [anywhere] * 4,
         out_specs=[anywhere] * 4,
         scratch_shapes=[
             V(slots, bf16), V(slots, bf16),
@@ -500,11 +505,12 @@
             V((2, LANES, HEAD), bf16), V((2, LANES, HEAD), bf16),
             V((2, WINDOW, LANES), f32), V((2, WINDOW, LANES), bf16),
             V((2, BACK + 3, BLOCK, HEAD), f32), V((2, BACK + 3, BLOCK, HEAD), f32),
+            V((1, NBLK), jnp.int32), pltpu.SMEM((1, NBLK), jnp.int32),
             V((2, 2, 4, 4, ZH) + piece, bf16), V((2, 2, 4, 4, ZH) + piece, bf16),
             V((2, 2, 4, 4, ZH) + piece, bf16), V((2, 2, 3, 4, ZH) + piece, bf16),
             V((2, 2, 4, ZH) + piece, bf16), V((2, 2, 3, ZH) + piece, bf16),
             V((2, ZH, 2) + piece, bf16),
-            dma((8,)),
+            dma((9,)),
             dma((2, 7)), dma((2, 7)),
             dma((2, 3)), dma((2, 3)),
             dma((2, 2, 3)), dma((2, 2, 3)),
@@ -520,7 +526,7 @@
             collective_id=0, has_side_effects=True, vmem_limit_bytes=VMEM_LIMIT
         ),
         name="fused",
-    )(doc_lengths, row_block, slot_of, queries, keys, values, out_grad)
+    )(doc_lengths, row_block, row_block.reshape(1, NBLK), queries, keys, values, out_grad)
 
 
 def hand_over_kernel(*refs):

time: 68.6 us -> 67.5 us (0.984)
  other arithmetic: 1.28 us -> 0 us
    reduce_sum x1 -> x0, other arithmetic: 1.28 us -> none  [fused(): slot_of = jnp.sum(jnp.where(found, number[None, :], 0), axis=1)]
where the time goes in v6:
time: 67.5 us; the launch traced here: 67.3 us
  Pallas kernels  66.5 us (99%)
  between operations  0.8 us (1%)
    pallas_call x1, Pallas kernels, fused(): pl.pallas_call(fused_kernel, out_shape=(jax.ShapeDtypeStruct((MINE, TP *...  64.7 us
    pallas_call x1, Pallas kernels, hand_over(): pl.pallas_call(hand_over_kernel, out_shape=tuple((jax.ShapeDtypeStruct(a....  1.82 us

profile of v6, /device:TPU:1, one launch (start us, length us, event | category | flops | bytes accessed | tf_op | source)
XLA Modules:
  0.0 67.3 jit_solution(1891461016729316266)
XLA Ops:
  0.6 64.7 %fused.1 = (bf16[32,4096]{1,0:T(8,128)(2,1)}, bf16[32,4096]{1,0:T(8,128)(2,1)}, bf16[2,4,32,128]{3,2,1,0:T(8,128)(2,1)}, bf16[2,4,32,128]{3,2,1,0:T(8,128)(2,1)}) custom-call(s32[16]{0:T(128)} %doc.1, s32[128]{0:T(128)} %row_block.1, s32[1,128]{1,0:T(1,128)} %bitcast.1, bf16[32,4096]{1,0:T(8,128)(2,1)} %q.1, bf16[32,512]{1,0:T(8,128)(2,1)} %k.1, ...), custom_call_target="tpu_custom_call" | custom-call | tf_op jit(solution)/shard_map/fused/pallas_call | solution.py:490
  65.4 1.8 %hand_over.1 = (bf16[32,4096]{1,0:T(8,128)(2,1)}, bf16[32,4096]{1,0:T(8,128)(2,1)}, bf16[32,512]{1,0:T(8,128)(2,1)}, bf16[32,512]{1,0:T(8,128)(2,1)}) custom-call(bf16[32,4096]{1,0:T(8,128)(2,1)} %get-tuple-element.8.refs_0_, bf16[32,4096]{1,0:T(8,128)(2,1)} %get-tuple-element.9.refs_1_, bf16[2,4,32,128]{3,2,1,0:T(8,128)(2,1)} %get-tuple-element.10.refs_2_, ...), custom_call_target="tpu_custom_call" | custom-call | tf_op jit(solution)/shard_map/hand_over/pallas_call | solution.py:553
